TPU v7x, 32 devices: a whole 2x2x4 slice. The times are simulated.
32 devices in a mesh: pipe: 4 (over y, core), ctx: 4 (over z), width: 2 (over x).
Axes of the slice: x: 2, y: 2, z: 4, core: 2. Of those that a mesh axis runs over, the one named last changes fastest.
Arguments:
- tokens: int32 [512], P('ctx'), may hold values from 0 to 511
- table: bfloat16 [512, 8192], P(None, 'width'), may hold values from -6 to 6
- boundary: bfloat16 [4, 2, 512, 8192], P('pipe', None, 'ctx', 'width'), may hold values from -24 to 24, as said below
- saved_in: bfloat16 [4, 512, 8192], P('pipe', 'ctx', 'width'), may hold values from -24 to 24, as said below
- loss_grad: bfloat16 [512, 8192], P('ctx', 'width'), may hold values from -6 to 6
- gain: float32 [4, 8192], P('pipe', 'width'), may hold values from 0.1 to 1.9
- skip: float32 [4, 8192], P('pipe', 'width'), may hold values from -4 to 4
- residue: float32 [4, 16, 8192], P('pipe', None, 'width'), may hold values from -1.5 to 1.5
- decay_rate: float32 [4, 16, 8192], P('pipe', None, 'width'), may hold values from 0.000390625 to 2, as said below
Outputs:
- segment_out: bfloat16 [4, 512, 8192], P('pipe', 'ctx', 'width')
- input_grad: bfloat16 [4, 512, 8192], P('pipe', 'ctx', 'width')
- gain_grad: float32 [4, 4, 8192], P('pipe', 'ctx', 'width')
- skip_grad: float32 [4, 4, 8192], P('pipe', 'ctx', 'width')
Inputs may be any that keep to these rules, and one draw needn't show every extreme that they name: `boundary`: activations and gradients stored from earlier steps. `saved_in`: a stored input. `decay_rate`: positive decays.
All inputs are finite; a program needn't handle non-finite values.
Results may differ from a plain program's by a relative error of at most 0.0034.
Values may be sent and summed in bfloat16 or wider, within the bound.
A program may use at most 128 MiB of HBM per device.

v0:
```python
import jax
import jax.numpy as jnp
import numpy as np
from jax import lax
from jax.sharding import PartitionSpec as P

D = 8192
BLK = 16


epsilon = 1e-06


def shifted(value, axis, steps):
    count = lax.axis_size(axis)
    initial, last = (max(0, -steps), min(count, count - steps))
    return lax.ppermute(value, axis, [(source, source + steps) for source in range(initial, last)])


def prefix(value, axis, join, neutral):
    count, mine = (lax.axis_size(axis), lax.axis_index(axis))
    pieces = jax.tree.map(lambda part: lax.all_gather(part, axis), value)
    total = jax.tree.map(
        lambda part, zero: jnp.full_like(part, 0) + jnp.asarray(zero, part.dtype), value, neutral
    )

    def hop(position, total):
        longer = join(total, jax.tree.map(lambda part: part[position], pieces))
        return jax.tree.map(lambda new, old: jnp.where(position < mine, new, old), longer, total)

    return lax.fori_loop(0, count - 1, hop, total)


def prefix_2(value, axis, combine, identity):
    peers, place = (lax.axis_size(axis), lax.axis_index(axis))
    everything = jax.tree.map(
        lambda part, kind: lax.all_gather(part.astype(kind), axis),
        value,
        (jnp.bfloat16, jnp.bfloat16),
    )
    start = jax.tree.map(
        lambda part, zero: jnp.broadcast_to(jnp.asarray(zero, part.dtype), part.shape),
        value,
        identity,
    )

    def hop(k, before):
        at = peers - 1 - k
        reached = at > place
        new = combine(
            before, jax.tree.map(lambda part, own: part[at].astype(own.dtype), everything, value)
        )
        return jax.tree.map(lambda a, b: jnp.where(reached, a, b), new, before)

    return lax.fori_loop(0, peers, hop, start)


def conv_tables(damping, scaled_residue, block_len):
    lags = jnp.arange(block_len, dtype=jnp.float32)
    decay_pow = jnp.exp(-damping[:, None, :] * lags[None, :, None])
    kernel = jnp.sum(scaled_residue[:, None, :] * decay_pow, axis=0)
    diff_index = np.maximum(np.arange(block_len)[:, None] - np.arange(block_len)[None, :], 0)
    lower_mask = (np.arange(block_len)[:, None] >= np.arange(block_len)[None, :]).astype(np.float32)
    toeplitz = (
        kernel[diff_index.reshape(-1)].reshape(block_len, block_len, -1)
        * jnp.asarray(lower_mask)[:, :, None]
    )
    tail = jnp.flip(decay_pow, 1)
    lead = scaled_residue[:, None, :] * decay_pow * jnp.exp(-damping)[:, None, :]
    stride = jnp.exp(-damping * float(block_len))
    return (toeplitz, tail, lead, stride)


def contract_lags(weights, pieces):
    block_count = pieces.shape[0]
    rows_out = weights.shape[0]
    channels = pieces.shape[2]

    def add_lag(lag_index, total):
        weight_col = lax.dynamic_index_in_dim(weights, lag_index, 1, keepdims=False)
        piece_col = lax.dynamic_index_in_dim(pieces, lag_index, 1, keepdims=False)
        return total + weight_col[None, :, :] * piece_col[:, None, :]

    return lax.fori_loop(
        0, weights.shape[1], add_lag, jnp.zeros((block_count, rows_out, channels), jnp.float32)
    )


def local_conv(signal, tables):
    toeplitz, tail, lead, stride = tables
    length, channels = signal.shape
    block_len = toeplitz.shape[0]
    pieces = signal.reshape(length // block_len, block_len, channels)
    output = contract_lags(toeplitz, pieces)
    summary = contract_lags(tail, pieces)

    def advance(state_now, block_sum):
        return (stride * state_now + block_sum, state_now)

    last_state, entries = lax.scan(advance, jnp.zeros(stride.shape, jnp.float32), summary)
    return (output, entries, last_state)


def finish_entering(output, entries, entering, tables):
    toeplitz, tail, lead, stride = tables
    block_count = entries.shape[0]
    block_len = toeplitz.shape[0]
    steps_before = jnp.arange(block_count, dtype=jnp.float32)[:, None, None]
    damping_blocks = -jnp.log(stride) / float(block_len)
    powers = jnp.exp(-damping_blocks[None] * (float(block_len) * steps_before))
    total_entries = entries + powers * entering[None]
    carried = contract_lags(jnp.transpose(lead, (1, 0, 2)), total_entries)
    total = output + carried
    return total.reshape(total.shape[0] * total.shape[1], total.shape[2])


def joiner(damping, length):

    def combine_states(earlier, later):
        factor = jnp.exp(-damping * (float(length) * later[0][0]))
        return (earlier[0] + later[0], factor * earlier[1] + later[1])

    return combine_states


def local(tokens, table, boundary, saved_in, loss_grad, gain, skip, residue, decay_rate):
    segment_index = lax.axis_index("pipe")
    segments = lax.axis_size("pipe")
    arrived = shifted(boundary[0, 1], "pipe", 1)
    returned = shifted(boundary[0, 0], "pipe", -1)
    onehot = (tokens[:, None] == jnp.arange(table.shape[0], dtype=jnp.int32)[None, :]).astype(
        jnp.bfloat16
    )
    embedded = jnp.dot(onehot, table, preferred_element_type=jnp.float32).astype(jnp.bfloat16)
    forward_in = jnp.where(segment_index == 0, embedded, arrived).astype(jnp.float32)
    cotangent = jnp.where(segment_index == segments - 1, loss_grad, returned).astype(jnp.float32)
    saved_rows = saved_in[0].astype(jnp.float32)
    square_sums = lax.psum(
        (jnp.sum(forward_in * forward_in, axis=1), jnp.sum(saved_rows * saved_rows, axis=1)),
        "width",
    )
    scale_fwd = lax.rsqrt(square_sums[0] / D + epsilon)[:, None]
    scale_back = lax.rsqrt(square_sums[1] / D + epsilon)[:, None]
    gain_row = gain[0]
    skip_row = skip[0]
    damping = decay_rate[0]
    scaled_residue = residue[0] * jnp.sqrt(1.0 - jnp.exp(-2.0 * damping))
    tables = conv_tables(damping, scaled_residue, BLK)
    normed_fwd = forward_in * scale_fwd * gain_row
    normed_back = saved_rows * scale_back * gain_row
    out_fwd, ent_fwd, last_fwd = local_conv(normed_fwd, tables)
    out_back, ent_back, last_back = local_conv(normed_back, tables)
    length = forward_in.shape[0]
    ends_local = jnp.stack([last_fwd, last_back])
    device_count = jnp.ones((1,), jnp.float32)
    neutral = (jnp.zeros((1,), jnp.float32), jnp.zeros_like(ends_local))
    counted, entering = prefix((device_count, ends_local), "ctx", joiner(damping, length), neutral)
    mixed_fwd = finish_entering(out_fwd, ent_fwd, entering[0], tables) + skip_row * normed_fwd
    mixed_back = finish_entering(out_back, ent_back, entering[1], tables) + skip_row * normed_back
    segment_out = (forward_in + normed_fwd * mixed_fwd).astype(jnp.bfloat16)
    grad_mix = cotangent * normed_back
    out_rev, ent_rev, last_rev = local_conv(jnp.flip(grad_mix, 0), tables)
    device_count_rev = jnp.ones((1,), jnp.float32)
    neutral_rev = (jnp.zeros((1,), jnp.float32), jnp.zeros_like(last_rev))
    counted_rev, entering_rev = prefix_2(
        (device_count_rev, last_rev), "ctx", joiner(damping, length), neutral_rev
    )
    back_term = jnp.flip(finish_entering(out_rev, ent_rev, entering_rev, tables), 0)
    grad_norm = cotangent * mixed_back + skip_row * grad_mix + back_term
    grad_scaled = grad_norm * gain_row
    inner_sum = lax.psum(jnp.sum(grad_scaled * saved_rows, axis=1), "width")[:, None]
    input_grad = (
        cotangent + scale_back * grad_scaled - saved_rows * scale_back**3 * inner_sum / D
    ).astype(jnp.bfloat16)
    gain_grad = jnp.sum(grad_norm * saved_rows * scale_back, axis=0)[None, None, :]
    skip_grad = jnp.sum(grad_mix * normed_back, axis=0)[None, None, :]
    return (segment_out[None], input_grad[None], gain_grad, skip_grad)


def solution(mesh):
    in_specs = (
        P("ctx"),
        P(None, "width"),
        P("pipe", None, "ctx", "width"),
        P("pipe", "ctx", "width"),
        P("ctx", "width"),
        P("pipe", "width"),
        P("pipe", "width"),
        P("pipe", None, "width"),
        P("pipe", None, "width"),
    )
    out_specs = (
        P("pipe", "ctx", "width"),
        P("pipe", "ctx", "width"),
        P("pipe", "ctx", "width"),
        P("pipe", "ctx", "width"),
    )
    return jax.shard_map(local, mesh=mesh, in_specs=in_specs, out_specs=out_specs, check_vma=False)
```

profile of v0, /device:TPU:6, one launch (start us, length us, event | category | flops | bytes accessed | tf_op | source)
XLA Modules:
  0.0 1051.8 jit_solution(17086032662116679111)
XLA Ops:
  27.2 6.7 copy_multiply_fusion
  33.8 11.9 %all-reduce.1 = bf16[4]{0:T(256)(128)(2,1)S(1)} all-reduce(bf16[4]{0:T(256)(128)(2,1)S(1)} %dynamic-update-slice.1), channel_id=1, replica_groups=mesh['pipe'=4,'ctx'=4,'width'=2] {'ctx'}, use_global_device_ids=true, to_apply=%add.1 | all-reduce | flops 4 | bytes 16
  45.8 8.4 all-reduce
  54.3 4.7 rev.11
  65.6 5.1 all-reduce.2
  77.7 79.4 %while.198 = (s32[]{:T(128)}, f32[8,16,4096]{2,1,0:T(8,128)}, f32[16,16,4096]{2,0,1:T(8,128)}, f32[8,16,4096]{2,0,1:T(8,128)}, s32[]{:T(128)}, /*index=5*/s32[]{:T(128)}) while((s32[]{:T(128)}, f32[8,16,4096]{2,1,0:T(8,128)}, f32[16,16,4096]{2,0,1:T(8,128)}, f32[8,16,4096]{2,0,1:T(8,128)}, s32[]{:T(128)}, ...), condition=%wide.region_6.7_spmd.clone, body=%wide.region_5.6_spmd.clone.sunk | while | flops 1572867 | bytes 5374039 | solution.py:84
  158.6 59.0 %while.199 = (s32[]{:T(128)}, f32[16,4096]{1,0:T(8,128)S(1)}, f32[8,16,4096]{2,0,1:T(8,128)}, f32[16,4096]{1,0:T(8,128)S(1)}, f32[8,16,4096]{2,1,0:T(8,128)}, /*index=5*/s32[]{:T(128)}, s32[]{:T(128)}) while((s32[]{:T(128)}, f32[16,4096]{1,0:T(8,128)S(1)}, f32[8,16,4096]{2,0,1:T(8,128)}, f32[16,4096]{1,0:T(8,128)S(1)}, ...), condition=%wide.region_8.9_spmd.clone, body=%wide.region_7.8_spmd.clone.sunk | while | flops 196611 | bytes 2359391 | solution.py:100
  160.0 6.0 dynamic_update_slice.16
  167.4 6.0 dynamic_update_slice.16
  174.8 6.0 dynamic_update_slice.16
  182.2 6.0 dynamic_update_slice.16
  189.5 6.0 dynamic_update_slice.16
  196.9 6.0 dynamic_update_slice.16
  204.3 6.0 dynamic_update_slice.16
  211.7 6.0 dynamic_update_slice.16
  221.9 78.9 %while.200 = (s32[]{:T(128)}, f32[8,16,4096]{2,1,0:T(8,128)}, f32[16,16,4096]{2,0,1:T(8,128)}, f32[8,16,4096]{2,0,1:T(8,128)}, s32[]{:T(128)}, /*index=5*/s32[]{:T(128)}) while((s32[]{:T(128)}, f32[8,16,4096]{2,1,0:T(8,128)}, f32[16,16,4096]{2,0,1:T(8,128)}, f32[8,16,4096]{2,0,1:T(8,128)}, s32[]{:T(128)}, ...), condition=%wide.region_12.13_spmd.clone, body=%wide.region_11.12_spmd.clone.sunk | while | flops 1572867 | bytes 5374039 | solution.py:84
  302.4 59.0 %while.201 = (s32[]{:T(128)}, f32[16,4096]{1,0:T(8,128)S(1)}, f32[8,16,4096]{2,0,1:T(8,128)}, f32[16,4096]{1,0:T(8,128)S(1)}, f32[8,16,4096]{2,1,0:T(8,128)}, /*index=5*/s32[]{:T(128)}, s32[]{:T(128)}) while((s32[]{:T(128)}, f32[16,4096]{1,0:T(8,128)S(1)}, f32[8,16,4096]{2,0,1:T(8,128)}, f32[16,4096]{1,0:T(8,128)S(1)}, ...), condition=%wide.region_14.15_spmd.clone, body=%wide.region_13.14_spmd.clone.sunk | while | flops 196611 | bytes 2359391 | solution.py:100
  303.8 6.0 dynamic_update_slice.17
  311.2 6.0 dynamic_update_slice.17
  318.6 6.0 dynamic_update_slice.17
  325.9 6.0 dynamic_update_slice.17
  333.3 6.0 dynamic_update_slice.17
  340.7 6.0 dynamic_update_slice.17
  348.1 6.0 dynamic_update_slice.17
  355.5 6.0 dynamic_update_slice.17
  362.3 16.7 %rev.12 = f32[128,4096]{1,0:T(8,128)} reverse(f32[128,4096]{1,0:T(8,128)} %get-tuple-element.1516), dimensions={0} | reverse | bytes 4194304 | tf_op jit(solution)/shard_map/jit(_flip)/rev | solution.py:162
  383.1 79.3 %while.207 = (s32[]{:T(128)}, f32[8,16,4096]{2,1,0:T(8,128)}, f32[16,16,4096]{2,0,1:T(8,128)}, f32[8,16,4096]{2,0,1:T(8,128)}, s32[]{:T(128)}, /*index=5*/s32[]{:T(128)}) while((s32[]{:T(128)}, f32[8,16,4096]{2,1,0:T(8,128)}, f32[16,16,4096]{2,0,1:T(8,128)}, f32[8,16,4096]{2,0,1:T(8,128)}, s32[]{:T(128)}, ...), condition=%wide.region_26.27_spmd.clone, body=%wide.region_25.26_spmd.clone.sunk | while | flops 1572867 | bytes 5374039 | solution.py:84
  464.0 59.0 %while.208 = (s32[]{:T(128)}, f32[16,4096]{1,0:T(8,128)S(1)}, f32[8,16,4096]{2,0,1:T(8,128)}, f32[16,4096]{1,0:T(8,128)S(1)}, f32[8,16,4096]{2,1,0:T(8,128)}, /*index=5*/s32[]{:T(128)}, s32[]{:T(128)}) while((s32[]{:T(128)}, f32[16,4096]{1,0:T(8,128)S(1)}, f32[8,16,4096]{2,0,1:T(8,128)}, f32[16,4096]{1,0:T(8,128)S(1)}, ...), condition=%wide.region_28.29_spmd.clone, body=%wide.region_27.28_spmd.clone.sunk | while | flops 196611 | bytes 2359391 | solution.py:100
  465.4 6.0 dynamic_update_slice.18
  472.8 6.0 dynamic_update_slice.18
  480.2 6.0 dynamic_update_slice.18
  487.5 6.0 dynamic_update_slice.18
  494.9 6.0 dynamic_update_slice.18
  502.3 6.0 dynamic_update_slice.18
  509.7 6.0 dynamic_update_slice.18
  517.0 6.0 dynamic_update_slice.18
  523.0 16.6 %all-gather.1 = bf16[64,4096]{1,0:T(8,128)(2,1)} all-gather(bf16[16,4096]{1,0:T(8,128)(2,1)S(1)} %convert_element_type.63), channel_id=3, replica_groups=mesh['pipe'=4,'ctx'=4,'width'=2] {'ctx'}, dimensions={0}, use_global_device_ids=true | all-gather | bytes 655360 | tf_op jit(solution)/shard_map/all_gather | solution.py:37
  539.6 80.3 %while.197 = (s32[]{:T(128)}, f32[8,16,4096]{2,1,0:T(8,128)}, f32[16,16,4096]{2,0,1:T(8,128)}, f32[8,16,4096]{2,0,1:T(8,128)}, s32[]{:T(128)}, /*index=5*/s32[]{:T(128)}) while((s32[]{:T(128)}, f32[8,16,4096]{2,1,0:T(8,128)}, f32[16,16,4096]{2,0,1:T(8,128)}, f32[8,16,4096]{2,0,1:T(8,128)}, s32[]{:T(128)}, ...), condition=%wide.region_4.5_spmd.clone, body=%wide.region_3.4_spmd.clone.sunk | while | flops 1572867 | bytes 5374039 | solution.py:84
  619.9 80.3 %while.204 = (s32[]{:T(128)}, f32[8,16,4096]{2,1,0:T(8,128)}, f32[16,16,4096]{2,0,1:T(8,128)}, f32[8,16,4096]{2,0,1:T(8,128)}, s32[]{:T(128)}, /*index=5*/s32[]{:T(128)}) while((s32[]{:T(128)}, f32[8,16,4096]{2,1,0:T(8,128)}, f32[16,16,4096]{2,0,1:T(8,128)}, f32[8,16,4096]{2,0,1:T(8,128)}, s32[]{:T(128)}, ...), condition=%wide.region_20.21_spmd.clone, body=%wide.region_19.20_spmd.clone.sunk | while | flops 1572867 | bytes 5374039 | solution.py:84
  700.2 79.8 %while.206 = (s32[]{:T(128)}, f32[8,16,4096]{2,1,0:T(8,128)}, f32[16,16,4096]{2,0,1:T(8,128)}, f32[8,16,4096]{2,0,1:T(8,128)}, s32[]{:T(128)}, /*index=5*/s32[]{:T(128)}) while((s32[]{:T(128)}, f32[8,16,4096]{2,1,0:T(8,128)}, f32[16,16,4096]{2,0,1:T(8,128)}, f32[8,16,4096]{2,0,1:T(8,128)}, s32[]{:T(128)}, ...), condition=%wide.region_24.25_spmd.clone, body=%wide.region_23.24_spmd.clone.sunk | while | flops 1572867 | bytes 5374039 | solution.py:84
  780.0 9.4 while.209
  789.5 10.7 %while.202 = (s32[]{:T(128)}, f32[2,16,4096]{2,1,0:T(8,128)S(1)}, s32[]{:T(128)}, f32[4,1]{0,1:T(1,128)S(1)}, f32[1,16,4096]{2,1,0:T(8,128)}, /*index=5*/f32[4,2,16,4096]{3,2,1,0:T(8,128)}, s32[]{:T(128)}, s32[]{:T(128)}) while((s32[]{:T(128)}, f32[2,16,4096]{2,1,0:T(8,128)S(1)}, s32[]{:T(128)}, f32[4,1]{0,1:T(1,128)S(1)}, ...), condition=%wide.region_16.17_spmd.clone, body=%wide.region_15.16_spmd.clone.sunk | while | flops 589829 | bytes 2359421 | solution.py:31
  800.2 6.2 multiply_add_fusion.1
  806.4 78.8 %while.203 = (s32[]{:T(128)}, f32[8,16,4096]{2,1,0:T(8,128)}, f32[16,16,4096]{2,0,1:T(8,128)}, f32[8,16,4096]{2,0,1:T(8,128)}, s32[]{:T(128)}, /*index=5*/s32[]{:T(128)}) while((s32[]{:T(128)}, f32[8,16,4096]{2,1,0:T(8,128)}, f32[16,16,4096]{2,0,1:T(8,128)}, f32[8,16,4096]{2,0,1:T(8,128)}, s32[]{:T(128)}, ...), condition=%wide.region_18.19_spmd.clone, body=%wide.region_17.18_spmd.clone.sunk | while | flops 1572867 | bytes 5374039 | solution.py:84
  885.2 79.3 %while.205 = (s32[]{:T(128)}, f32[8,16,4096]{2,1,0:T(8,128)}, f32[16,16,4096]{2,0,1:T(8,128)}, f32[8,16,4096]{2,0,1:T(8,128)}, s32[]{:T(128)}, /*index=5*/s32[]{:T(128)}) while((s32[]{:T(128)}, f32[8,16,4096]{2,1,0:T(8,128)}, f32[16,16,4096]{2,0,1:T(8,128)}, f32[8,16,4096]{2,0,1:T(8,128)}, s32[]{:T(128)}, ...), condition=%wide.region_22.23_spmd.clone, body=%wide.region_21.22_spmd.clone.sunk | while | flops 1572867 | bytes 5374039 | solution.py:84
  964.5 41.6 %while.210 = (s32[]{:T(128)}, f32[8,16,4096]{2,1,0:T(8,128)S(1)}, f32[16,16,4096]{2,0,1:T(8,128)}, f32[8,16,4096]{2,0,1:T(8,128)}, s32[]{:T(128)}, /*index=5*/s32[]{:T(128)}) while((s32[]{:T(128)}, f32[8,16,4096]{2,1,0:T(8,128)S(1)}, f32[16,16,4096]{2,0,1:T(8,128)}, f32[8,16,4096]{2,0,1:T(8,128)}, s32[]{:T(128)}, ...), condition=%wide.region_32.33_spmd.clone, body=%wide.region_31.32_spmd.clone.sunk | while | flops 1572867 | bytes 5374039 | solution.py:84
  1009.2 16.6 %rev.13 = f32[128,4096]{1,0:T(8,128)} reverse(f32[128,4096]{1,0:T(8,128)} %bitcast.204), dimensions={0} | reverse | bytes 4194304 | tf_op jit(solution)/shard_map/jit(_flip)/rev | solution.py:168
  1036.6 4.9 psum.23
  (599 shorter events, 793.5 us)
Async XLA Ops:
  7.2 8.9 copy-start.15
  7.2 9.0 copy-start.18
  7.2 782.3 %all-gather.4.cloned.1.call-start = ((), (), s32[]{:S(2)}) async-start(), calls=%async_computation | async-start | bytes 2621440 | tf_op jit(solution)/shard_map/all_gather | solution.py:22
  10.4 6.8 copy-start.22
  10.4 6.8 copy-start.23
  10.4 50.5 %collective-permute-start = (bf16[128,4096]{1,0:T(8,128)(2,1)}, bf16[128,4096]{1,0:T(8,128)(2,1)}, u32[]{:S(2)}, u32[]{:S(2)}) collective-permute-start(bf16[128,4096]{1,0:T(8,128)(2,1)} %get-tuple-element.1525), channel_id=1, source_target_pairs={{0,8},{8,16},{16,24},{1,9},{9,17},{17,25},{2,10},{10,18},{18,26},{... | collective-permute-start | bytes 3145736 | tf_op jit(solution)/shard_map/ppermute | solution.py:17
  12.4 58.4 %collective-permute-start.1 = (bf16[128,4096]{1,0:T(8,128)(2,1)}, bf16[128,4096]{1,0:T(8,128)(2,1)}, u32[]{:S(2)}, u32[]{:S(2)}) collective-permute-start(bf16[128,4096]{1,0:T(8,128)(2,1)} %get-tuple-element.1524), channel_id=1, source_target_pairs={{8,0},{16,8},{24,16},{9,1},{17,9},{25,17},{10,2},{18,10},{26,18},{... | collective-permute-start | bytes 3145736 | tf_op jit(solution)/shard_map/ppermute | solution.py:17
  17.1 6.2 copy-start.6
  23.3 3.9 copy-start.20
  54.3 4.7 copy-start.2
  59.0 1.9 copy-start.21
  60.9 9.9 copy-start.17
  157.1 1.5 copy-start.11
  300.8 1.6 copy-start.10
  462.4 1.6 copy-start.9
  700.2 79.8 %copy-start.7 = (f32[16,4096]{1,0:T(8,128)S(1)}, f32[16,4096]{1,0:T(8,128)}, u32[]{:S(2)}) copy-start(f32[16,4096]{1,0:T(8,128)} %copy-done.6) | copy-start | bytes 786436
  700.2 79.8 %copy-start.8 = (f32[16,4096]{1,0:T(8,128)S(1)}, f32[16,4096]{1,0:T(8,128)}, u32[]{:S(2)}) copy-start(f32[16,4096]{1,0:T(8,128)} %custom-call.12) | copy-start | bytes 786436
  780.0 9.4 copy-start.5
  789.5 10.8 %copy-start.16 = (f32[16,4096]{1,0:T(8,128)S(1)}, f32[16,4096]{1,0:T(8,128)}, u32[]{:S(2)}) copy-start(f32[16,4096]{1,0:T(8,128)} %get-tuple-element.1533) | copy-start | bytes 786436
  1025.9 2.9 copy-start
  1025.9 3.5 copy-start.1
  1025.9 3.8 copy-start.19
  1029.4 1.2 copy-start.3
  1029.4 1.9 copy-start.4
  1029.4 2.2 copy-start.12
  1029.4 2.9 copy-start.14
  1032.2 9.3 copy-start.13
Sparse Core Ops, SparseCore 0:
  362.4 45.5 all-gather.3
where the time goes:
time: 1070 us; the launch traced here: 1050 us
  other arithmetic  493 us (46%)
  local copies, waits for them, and re-layouts  484 us (45%)
  blocking collectives  46.9 us (4%)
  between operations  14.4 us (1%)
    add x144, other arithmetic, add_lag(): return total + weight_col[None, :, :] * piece_col[:, None, :]  404 us
    mul x288, local copies, waits for them, and re-layouts, add_lag(): return total + weight_col[None, :, :] * piece_col[:, None, :]  272 us
    dynamic_update_slice x48, local copies, waits for them, and re-layouts, local_conv(): lax.scan(advance, jnp.zeros(stride.shape, jnp.float32), summary)  150 us
    broadcast_in_dim x24, other arithmetic, local_conv(): lax.scan(advance, jnp.zeros(stride.shape, jnp.float32), summary)  26.6 us
  transfers between devices with their start and end apart: 3, of which 0 were waited for; matrix products, arithmetic and copies ran while one was open for 42% of the time, Pallas kernels for 0%

commit v1 on v0

v1 whole, which is shorter than its diff:
```python
import jax
import jax.numpy as jnp
from jax import lax
from jax.experimental import pallas as pl
from jax.experimental.pallas import tpu as pltpu
from jax.sharding import PartitionSpec as P

D = 8192
ROWS = 8
LANES = 128
CHUNK = 512
epsilon = 1e-06


def shifted(value, axis, steps):
    count = lax.axis_size(axis)
    initial, last = (max(0, -steps), min(count, count - steps))
    return lax.ppermute(value, axis, [(source, source + steps) for source in range(initial, last)])


def width_sum(value):
    if lax.axis_size("width") == 2:
        return value + lax.ppermute(value, "width", [(0, 1), (1, 0)])
    return lax.psum(value, "width")


def wide(row):
    return jnp.broadcast_to(row, (ROWS, LANES))


def states_kernel(x_ref, sav_ref, cot_ref, sf_ref, sb_ref, gain_ref, decay_ref,
                  e_ref, end_ref, sig, last):
    length = x_ref.shape[0]
    steps = length // ROWS
    modes = decay_ref.shape[0]
    place = lax.broadcasted_iota(jnp.int32, (ROWS, LANES), 0)

    def group(g, carry):
        lanes = pl.ds(pl.multiple_of(g * LANES, LANES), LANES)
        gain = gain_ref[:, lanes]
        back = sav_ref[:, lanes].astype(jnp.float32) * sb_ref[...] * gain
        sig[0] = x_ref[:, lanes].astype(jnp.float32) * sf_ref[...] * gain
        sig[1] = back
        sig[2] = cot_ref[:, lanes].astype(jnp.float32) * back
        damping = decay_ref[:, lanes]
        a_all = jnp.exp(-damping)
        stride_all = jnp.exp(-damping * float(steps))
        a = [wide(a_all[k:k + 1]) for k in range(modes)]
        for q in range(3):
            rev = q == 2
            order = range(steps - 1, -1, -1) if rev else range(steps)
            state = None
            for j in order:
                piece = sig[q, pl.ds(j, ROWS, stride=steps), :]
                if state is None:
                    state = [piece] * modes
                else:
                    state = [a[k] * state[k] + piece for k in range(modes)]
            for k in range(modes):
                power = wide(stride_all[k:k + 1])
                total = state[k]
                hop = 1
                while hop < ROWS:
                    near = (place < ROWS - hop) if rev else (place >= hop)
                    moved = pltpu.roll(total, ROWS - hop if rev else hop, 0)
                    total = total + jnp.where(near, power * moved, 0.0)
                    power = power * power
                    hop *= 2
                near = (place < ROWS - 1) if rev else (place >= 1)
                moved = pltpu.roll(total, ROWS - 1 if rev else 1, 0)
                e_ref[q, k, :, lanes] = jnp.where(near, moved, 0.0)
                edge = 0 if rev else ROWS - 1
                last[k:k + 1, :] = total[edge:edge + 1, :]
            end_ref[q, :, lanes] = last[...].astype(end_ref.dtype)
        return carry

    lax.fori_loop(0, x_ref.shape[1] // LANES, group, 0)


def finish_kernel(mine_ref, x_ref, sav_ref, cot_ref, sf_ref, sb_ref, gain_ref, skip_ref,
                  residue_ref, decay_ref, e_ref, ends_ref,
                  out_ref, part_ref, gg_ref, sg_ref, acc_ref, sig, res):
    length = x_ref.shape[0]
    steps = length // ROWS
    modes = decay_ref.shape[0]
    peers = ends_ref.shape[0]
    mine = mine_ref[0]
    place = lax.broadcasted_iota(jnp.int32, (ROWS, LANES), 0).astype(jnp.float32)

    @pl.when(pl.program_id(0) == 0)
    def _():
        acc_ref[...] = jnp.zeros_like(acc_ref)

    def group(g, carry):
        lanes = pl.ds(pl.multiple_of(g * LANES, LANES), LANES)
        gain = gain_ref[:, lanes]
        gain_w = wide(gain)
        sig[0] = x_ref[:, lanes].astype(jnp.float32)
        sig[1] = sav_ref[:, lanes].astype(jnp.float32) * sb_ref[...]
        sig[2] = cot_ref[:, lanes].astype(jnp.float32)
        damping = decay_ref[:, lanes]
        a_all = jnp.exp(-damping)
        coefs = residue_ref[:, lanes] * jnp.sqrt(1.0 - jnp.exp(-2.0 * damping))
        whole = jnp.exp(-damping * float(length))
        entering = []
        for q in range(3):
            total = jnp.zeros((modes, LANES), jnp.float32)
            for hop in range(peers - 1):
                at = peers - 1 - hop if q == 2 else hop
                reached = (at > mine) if q == 2 else (at < mine)
                longer = whole * total + ends_ref[at, q, :, lanes].astype(jnp.float32)
                total = jnp.where(reached, longer, total)
            entering.append(total)
        kernel = []
        power = coefs
        for n in range(steps):
            kernel.append(wide(jnp.sum(power, axis=0, keepdims=True)))
            power = power * a_all
        kernel[0] = kernel[0] + wide(skip_ref[:, lanes])

        def rows(i):
            return pl.ds(i, ROWS, stride=steps)

        def conv(q, pieces, emit):
            rev = q == 2
            ago = (float(ROWS - 1) - place) if rev else place
            decayed = []
            for k in range(modes):
                gap = jnp.exp(wide(damping[k:k + 1]) * (ago * float(-steps)))
                state = e_ref[q, k, :, lanes] + gap * wide(entering[q][k:k + 1])
                decayed.append(wide(coefs[k:k + 1]) * state)
            a = [wide(a_all[k:k + 1]) for k in range(modes)]
            for n in range(steps):
                decayed = [a[k] * decayed[k] for k in range(modes)]
                terms = decayed + [kernel[n - m] * pieces[steps - 1 - m if rev else m]
                                   for m in range(n + 1)]
                sums = terms[:4]
                for index, term in enumerate(terms[4:]):
                    sums[index % 4] = sums[index % 4] + term
                emit(steps - 1 - n if rev else n, (sums[0] + sums[1]) + (sums[2] + sums[3]))

        raw = [sig[0, rows(i), :] for i in range(steps)]
        normed = [raw[i] * sf_ref[rows(i), :] * gain_w for i in range(steps)]

        def emit_out(i, value):
            res[0, rows(i), :] = sig[0, rows(i), :] + sig[0, rows(i), :] * sf_ref[rows(i), :] * gain_w * value

        conv(0, normed, emit_out)
        out_ref[:, lanes] = res[0].astype(out_ref.dtype)

        back = [sig[1, rows(i), :] * gain_w for i in range(steps)]

        def emit_mixed(i, value):
            res[1, rows(i), :] = sig[2, rows(i), :] * value

        conv(1, back, emit_mixed)

        mix = [sig[2, rows(i), :] * back[i] for i in range(steps)]
        skip_sum = mix[0] * back[0]
        for i in range(1, steps):
            skip_sum = skip_sum + mix[i] * back[i]
        sg_ref[:, lanes] = jnp.sum(skip_sum, axis=0, keepdims=True)
        gain_sums = [jnp.zeros((ROWS, LANES), jnp.float32)]

        def emit_grad(i, value):
            norm = res[1, rows(i), :] + value
            unit = sig[1, rows(i), :]
            gain_sums[0] = gain_sums[0] + norm * unit
            scaled = gain_w * norm
            acc_ref[i] = acc_ref[i] + scaled * unit
            res[2, rows(i), :] = sig[2, rows(i), :] + sb_ref[rows(i), :] * scaled

        conv(2, mix, emit_grad)
        part_ref[:, lanes] = res[2]
        gg_ref[:, lanes] = jnp.sum(gain_sums[0], axis=0, keepdims=True)
        return carry

    lax.fori_loop(0, x_ref.shape[1] // LANES, group, 0)


def local(tokens, table, boundary, saved_in, loss_grad, gain, skip, residue, decay_rate):
    segment_index = lax.axis_index("pipe")
    segments = lax.axis_size("pipe")
    arrived = shifted(boundary[0, 1], "pipe", 1)
    returned = shifted(boundary[0, 0], "pipe", -1)
    onehot = (tokens[:, None] == jnp.arange(table.shape[0], dtype=jnp.int32)[None, :]).astype(
        jnp.bfloat16
    )
    embedded = jnp.dot(onehot, table, preferred_element_type=jnp.float32).astype(jnp.bfloat16)
    x = jnp.where(segment_index == 0, embedded, arrived)
    cot = jnp.where(segment_index == segments - 1, loss_grad, returned)
    sav = saved_in[0]
    x32, sav32 = x.astype(jnp.float32), sav.astype(jnp.float32)
    squares = width_sum(jnp.stack([jnp.sum(x32 * x32, axis=1), jnp.sum(sav32 * sav32, axis=1)]))
    scales = lax.rsqrt(squares / D + epsilon)
    length, channels = x.shape
    modes = decay_rate.shape[1]
    steps = length // ROWS
    sf = jnp.broadcast_to(scales[0][:, None], (length, LANES))
    sb = jnp.broadcast_to(scales[1][:, None], (length, LANES))
    chunk = min(CHUNK, channels)
    grid = (channels // chunk,)
    tall = pl.BlockSpec((length, chunk), lambda c: (0, c))
    scale_spec = pl.BlockSpec((length, LANES), lambda c: (0, 0))
    row = pl.BlockSpec((1, chunk), lambda c: (0, c))
    mode_spec = pl.BlockSpec((modes, chunk), lambda c: (0, c))
    e_spec = pl.BlockSpec((3, modes, ROWS, chunk), lambda c: (0, 0, 0, c))
    params = pltpu.CompilerParams(vmem_limit_bytes=40 * 1024 * 1024)
    f32 = jnp.float32
    work = length * channels
    entries, ends = pl.pallas_call(
        states_kernel,
        grid=grid,
        in_specs=[tall, tall, tall, scale_spec, scale_spec, row, mode_spec],
        out_specs=[e_spec, pl.BlockSpec((3, modes, chunk), lambda c: (0, 0, c))],
        out_shape=[
            jax.ShapeDtypeStruct((3, modes, ROWS, channels), f32),
            jax.ShapeDtypeStruct((3, modes, channels), jnp.bfloat16),
        ],
        scratch_shapes=[pltpu.VMEM((3, length, LANES), f32), pltpu.VMEM((modes, LANES), f32)],
        compiler_params=params,
        cost_estimate=pl.CostEstimate(flops=96 * work, bytes_accessed=18 * work, transcendentals=0),
    )(x, sav, cot, sf, sb, gain, decay_rate[0])
    gathered = lax.all_gather(ends, "ctx")
    mine = lax.axis_index("ctx").astype(jnp.int32).reshape(1)
    out, part, gain_grad, skip_grad, inner = pl.pallas_call(
        finish_kernel,
        grid=grid,
        in_specs=[
            pl.BlockSpec(memory_space=pltpu.SMEM), tall, tall, tall, scale_spec, scale_spec,
            row, row, mode_spec, mode_spec, e_spec,
            pl.BlockSpec((gathered.shape[0], 3, modes, chunk), lambda c: (0, 0, 0, c)),
        ],
        out_specs=[tall, tall, row, row, pl.BlockSpec((steps, ROWS, LANES), lambda c: (0, 0, 0))],
        out_shape=[
            jax.ShapeDtypeStruct((length, channels), jnp.bfloat16),
            jax.ShapeDtypeStruct((length, channels), f32),
            jax.ShapeDtypeStruct((1, channels), f32),
            jax.ShapeDtypeStruct((1, channels), f32),
            jax.ShapeDtypeStruct((steps, ROWS, LANES), f32),
        ],
        scratch_shapes=[pltpu.VMEM((3, length, LANES), f32), pltpu.VMEM((3, length, LANES), f32)],
        compiler_params=params,
        cost_estimate=pl.CostEstimate(flops=150 * work, bytes_accessed=24 * work, transcendentals=0),
    )(mine, x, sav, cot, sf, sb, gain, skip, residue[0], decay_rate[0], entries, gathered)
    inner_sum = width_sum(jnp.sum(inner, axis=2)).T.reshape(length)
    factor = (scales[1] ** 2 * inner_sum / D)[:, None]
    input_grad = (part - sav32 * factor).astype(jnp.bfloat16)
    return (out[None], input_grad[None], gain_grad[None], skip_grad[None])


def solution(mesh):
    in_specs = (
        P("ctx"),
        P(None, "width"),
        P("pipe", None, "ctx", "width"),
        P("pipe", "ctx", "width"),
        P("ctx", "width"),
        P("pipe", "width"),
        P("pipe", "width"),
        P("pipe", None, "width"),
        P("pipe", None, "width"),
    )
    out_specs = (
        P("pipe", "ctx", "width"),
        P("pipe", "ctx", "width"),
        P("pipe", "ctx", "width"),
        P("pipe", "ctx", "width"),
    )
    return jax.shard_map(local, mesh=mesh, in_specs=in_specs, out_specs=out_specs, check_vma=False)
```

time: 1070 us -> 134 us (0.13)
  the two profiles are of different devices: /device:TPU:6 before, /device:TPU:1 now
where the time goes in v1:
time: 134 us; the launch traced here: 131 us
  waiting for transfers between devices  51 us (38%)
  Pallas kernels  33.5 us (25%)
  between operations  14.2 us (11%)
  local copies, waits for them, and re-layouts  13.8 us (10%)
  starting transfers between devices  9.03 us (7%)
  other arithmetic  6.13 us (5%)
  matrix products  3.53 us (3%)
    all_gather x1, waiting for transfers between devices, local(): gathered = lax.all_gather(ends, 'ctx')  40.2 us
    pallas_call x1, Pallas kernels, local(): pl.pallas_call(finish_kernel, grid=grid, in_specs=[pl.BlockSpec(memory_sp...  21.4 us
    pallas_call x1, Pallas kernels, local(): pl.pallas_call(states_kernel, grid=grid, in_specs=[tall, tall, tall, scal...  12.1 us
    unnamed x28, local copies, waits for them, and re-layouts  11.7 us
    ppermute x2, waiting for transfers between devices, shifted(): lax.ppermute(value, axis, [(source, source + steps) for source in range(i...  9.48 us
    ppermute x2, starting transfers between devices, shifted(): lax.ppermute(value, axis, [(source, source + steps) for source in range(i...  6.46 us
    dot_general x1, matrix products, local(): jnp.dot(onehot, table, preferred_element_type=jnp.float32)  3.53 us
    broadcast_in_dim x1, other arithmetic, local(): return (out[None], input_grad[None], gain_grad[None], skip_grad[None])  2.89 us
  transfers between devices with their start and end apart: 5, of which 3 were waited for; matrix products, arithmetic and copies ran while one was open for 4% of the time, Pallas kernels for 0%

profile of v1, /device:TPU:1, one launch (start us, length us, event | category | flops | bytes accessed | tf_op | source)
XLA Modules:
  0.0 131.2 jit_solution(13384270886477799374)
XLA Ops:
  7.2 0.0 copy-start
  7.2 0.0 copy-start.13
  7.2 0.0 all-gather.3.cloned.1.call-start
  7.2 1.8 %slice_bitcast_fusion = (bf16[128,4096]{1,0:T(8,128)(2,1)S(1)}, bf16[128,4096]{1,0:T(8,128)(2,1)S(1)}) fusion(bf16[1,2,128,4096]{3,2,1,0:T(8,128)(2,1)} %param.11), kind=kLoop, calls=%fused_computation.9 | loop fusion | bytes 4194304 | tf_op jit(solution)/shard_map/squeeze | solution.py:185
  9.0 4.5 %collective-permute-start = (bf16[128,4096]{1,0:T(8,128)(2,1)S(1)}, bf16[128,4096]{1,0:T(8,128)(2,1)}, u32[]{:S(2)}, u32[]{:S(2)}) collective-permute-start(bf16[128,4096]{1,0:T(8,128)(2,1)S(1)} %get-tuple-element.19), channel_id=1, source_target_pairs={{0,8},{8,16},{16,24},{1,9},{9,17},{17,25},{2,10},{10,18},{18,26},{... | collective-permute-start | bytes 3145736 | tf_op jit(solution)/shard_map/ppermute | solution.py:18
  13.6 1.9 %collective-permute-start.1 = (bf16[128,4096]{1,0:T(8,128)(2,1)S(1)}, bf16[128,4096]{1,0:T(8,128)(2,1)}, u32[]{:S(2)}, u32[]{:S(2)}) collective-permute-start(bf16[128,4096]{1,0:T(8,128)(2,1)S(1)} %get-tuple-element.18), channel_id=1, source_target_pairs={{8,0},{16,8},{24,16},{9,1},{17,9},{25,17},{10,2},{18,10},{26,18},{... | collective-permute-start | bytes 3145736 | tf_op jit(solution)/shard_map/ppermute | solution.py:18
  15.5 0.0 copy-done
  15.5 0.3 fusion.1
  15.8 0.0 copy-start.11
  15.8 9.5 %collective-permute-done = bf16[128,4096]{1,0:T(8,128)(2,1)} collective-permute-done((bf16[128,4096]{1,0:T(8,128)(2,1)S(1)}, bf16[128,4096]{1,0:T(8,128)(2,1)}, u32[]{:S(2)}, u32[]{:S(2)}) %collective-permute-start) | collective-permute-done | bytes 1048608 | tf_op jit(solution)/shard_map/ppermute | solution.py:18
  25.3 0.0 copy-done.13
  25.3 3.5 %multiply_reduce_fusion = (f32[128]{0:T(128)S(1)}, bf16[128,4096]{1,0:T(8,128)(2,1)S(1)}) fusion(bf16[128,4096]{1,0:T(8,128)(2,1)} %collective-permute-done, bf16[512,4096]{1,0:T(8,128)(2,1)} %param.10, s32[128]{0:T(128)S(1)} %copy-done.13, pred[]{:T(512)S(6)} %eq.19), kind=kOutput, calls=%fused_computation.7 | convolution fusion | flops 539557760 | bytes 6292481 | tf_op jit(solution)/shard_map/dot_general | solution.py:189
  28.8 0.0 copy-start.5
  28.8 0.0 copy-start.8
  28.9 1.3 collective-permute-start.2
  30.1 0.0 collective-permute-done.1
  30.2 0.0 copy-done.11
  30.2 1.3 %broadcast_select_fusion.cot_ref = bf16[128,4096]{1,0:T(8,128)(2,1)S(1)} fusion(bf16[128,4096]{1,0:T(8,128)(2,1)S(1)} %copy-done.11, bf16[128,4096]{1,0:T(8,128)(2,1)} %collective-permute-done.1, pred[]{:T(512)S(6)} %eq.23), kind=kLoop, calls=%fused_computation.11 | loop fusion | flops 524288 | bytes 3145729 | tf_op jit(solution)/shard_map/jit(_where)/select_n | solution.py:191
  31.5 0.0 collective-permute-done.2
  31.5 0.0 copy-start.12
  31.5 0.1 broadcast_in_dim.32.sb_ref
  31.6 0.5 copy-done.12
  32.1 0.1 broadcast_in_dim.30.sf_ref
  32.2 0.0 copy-done.5
  32.2 0.0 copy-done.8
  32.2 12.1 %shard_map.120 = (f32[3,16,8,4096]{3,2,1,0:T(8,128)S(1)}, bf16[3,16,4096]{2,1,0:T(8,128)(2,1)S(1)}) custom-call(bf16[128,4096]{1,0:T(8,128)(2,1)S(1)} %get-tuple-element.23.x_ref, bf16[128,4096]{1,0:T(8,128)(2,1)S(1)} %bitcast.27, bf16[128,4096]{1,0:T(8,128)(2,1)S(1)} %broadcast_select_fusion.cot_ref, f32[128,128]{1,0:T(8,128)S(1)} %broadcast_in_dim.30.sf_ref, ...), custom_call_target="tpu_custom_call" | custom-call | flops 50331648 | bytes 9437184 | tf_op jit(solution)/shard_map/pallas_call | solution.py:211
  44.3 0.0 copy-start.1
  44.4 2.7 %copy-done.1 = f32[3,16,8,4096]{3,2,1,0:T(8,128)} copy-done((f32[3,16,8,4096]{3,2,1,0:T(8,128)}, f32[3,16,8,4096]{3,2,1,0:T(8,128)S(1)}, u32[]{:S(2)}) %copy-start.1) | copy-done | bytes 6291480
  47.0 0.0 copy-start.6
  47.0 0.7 copy-done.6
  47.8 0.0 all-gather.3.cloned.1.call-update
  47.8 40.2 %all-gather.3.cloned.1.call-done = bf16[12,16,4096]{2,1,0:T(8,128)(2,1)} async-done(((bf16[3,16,4096]{2,1,0:T(8,128)(2,1)}), bf16[12,16,4096]{2,1,0:T(8,128)(2,1)}) %all-gather.3.cloned.1.call-update) | async-done | bytes 1572880 | tf_op jit(solution)/shard_map/all_gather | solution.py:224
  87.9 0.0 copy-start.2
  88.0 2.8 %copy-done.2 = f32[3,16,8,4096]{3,2,1,0:T(8,128)S(1)} copy-done((f32[3,16,8,4096]{3,2,1,0:T(8,128)S(1)}, f32[3,16,8,4096]{3,2,1,0:T(8,128)}, u32[]{:S(2)}) %copy-start.2) | copy-done | bytes 6291480
  90.7 0.0 copy-start.4
  90.7 1.4 %copy-done.4 = bf16[12,16,4096]{2,1,0:T(8,128)(2,1)S(1)} copy-done((bf16[12,16,4096]{2,1,0:T(8,128)(2,1)S(1)}, bf16[12,16,4096]{2,1,0:T(8,128)(2,1)}, u32[]{:S(2)}) %copy-start.4) | copy-done | bytes 1572888
  92.1 0.9 copy-done.7
  93.1 0.7 copy-done.10
  93.8 21.4 %shard_map.121 = (bf16[128,4096]{1,0:T(8,128)(2,1)}, f32[128,4096]{1,0:T(8,128)S(1)}, f32[1,4096]{1,0:T(1,128)}, f32[1,4096]{1,0:T(1,128)}, f32[16,8,128]{2,1,0:T(8,128)S(1)}) custom-call(s32[1]{0:T(128)} %bitcast.mine_ref, bf16[128,4096]{1,0:T(8,128)(2,1)S(1)} %get-tuple-element.23.x_ref, bf16[128,4096]{1,0:T(8,128)(2,1)S(1)} %bitcast.28, ...), custom_call_target="tpu_custom_call" | custom-call | flops 78643200 | bytes 12582912 | tf_op jit(solution)/shard_map/pallas_call | solution.py:226
  115.2 1.3 %copy-done.3 = f32[128,4096]{1,0:T(8,128)} copy-done((f32[128,4096]{1,0:T(8,128)}, f32[128,4096]{1,0:T(8,128)S(1)}, u32[]{:S(2)}) %copy-start.3) | copy-done | bytes 2097176
  116.5 0.6 copy-done.9
  117.1 0.9 reduce_sum.29
  118.1 1.3 collective-permute-start.3
  119.3 1.3 %collective-permute-done.3 = f32[16,8]{1,0:T(8,128)S(1)} collective-permute-done((f32[16,8]{1,0:T(8,128)S(1)}, f32[16,8]{1,0:T(8,128)S(1)}, u32[]{:S(2)}, u32[]{:S(2)}) %collective-permute-start.3) | collective-permute-done | bytes 544 | tf_op jit(solution)/shard_map/ppermute | solution.py:23
  120.6 0.1 copy.13
  120.7 0.1 reshape.29
  120.8 0.7 multiply_multiply_fusion
  121.5 2.9 %fusion.4 = bf16[1,128,4096]{2,1,0:T(8,128)(2,1)} fusion(f32[128,4096]{1,0:T(8,128)} %copy-done.3, f32[128]{0:T(128)S(1)} %multiply_multiply_fusion, bf16[1,128,4096]{2,1,0:T(8,128)(2,1)S(1)} %copy-done), kind=kLoop, calls=%fused_computation.8 | loop fusion | flops 2097152 | bytes 4194816 | tf_op jit(solution)/shard_map/broadcast_in_dim | solution.py:249
  (8 shorter events, 0.0 us)
Async XLA Ops:
  7.2 8.4 %copy-start = (bf16[1,128,4096]{2,1,0:T(8,128)(2,1)S(1)}, bf16[1,128,4096]{2,1,0:T(8,128)(2,1)}, u32[]{:S(2)}) copy-start(bf16[1,128,4096]{2,1,0:T(8,128)(2,1)} %param.12) | copy-start | bytes 3145732
  7.2 18.1 %copy-start.13 = (s32[128]{0:T(128)S(1)}, s32[128]{0:T(128)}, u32[]{:S(2)}) copy-start(s32[128]{0:T(128)} %param.9) | copy-start | bytes 1540
  7.2 80.8 %all-gather.3.cloned.1.call-start = ((), (), s32[]{:S(2)}) async-start(), calls=%async_computation | async-start | bytes 1966080 | tf_op jit(solution)/shard_map/all_gather | solution.py:224
  9.0 16.3 %collective-permute-start = (bf16[128,4096]{1,0:T(8,128)(2,1)S(1)}, bf16[128,4096]{1,0:T(8,128)(2,1)}, u32[]{:S(2)}, u32[]{:S(2)}) collective-permute-start(bf16[128,4096]{1,0:T(8,128)(2,1)S(1)} %get-tuple-element.19), channel_id=1, source_target_pairs={{0,8},{8,16},{16,24},{1,9},{9,17},{17,25},{2,10},{10,18},{18,26},{... | collective-permute-start | bytes 3145736 | tf_op jit(solution)/shard_map/ppermute | solution.py:18
  13.6 16.6 %collective-permute-start.1 = (bf16[128,4096]{1,0:T(8,128)(2,1)S(1)}, bf16[128,4096]{1,0:T(8,128)(2,1)}, u32[]{:S(2)}, u32[]{:S(2)}) collective-permute-start(bf16[128,4096]{1,0:T(8,128)(2,1)S(1)} %get-tuple-element.18), channel_id=1, source_target_pairs={{8,0},{16,8},{24,16},{9,1},{17,9},{25,17},{10,2},{18,10},{26,18},{... | collective-permute-start | bytes 3145736 | tf_op jit(solution)/shard_map/ppermute | solution.py:18
  15.8 14.3 %copy-start.11 = (bf16[128,4096]{1,0:T(8,128)(2,1)S(1)}, bf16[128,4096]{1,0:T(8,128)(2,1)}, u32[]{:S(2)}) copy-start(bf16[128,4096]{1,0:T(8,128)(2,1)} %param.13) | copy-start | bytes 3145732
  28.8 3.3 %copy-start.5 = (f32[1,16,4096]{2,1,0:T(8,128)S(1)}, f32[1,16,4096]{2,1,0:T(8,128)}, u32[]{:S(2)}) copy-start(f32[1,16,4096]{2,1,0:T(8,128)} %param.17) | copy-start | bytes 786436
  28.8 3.3 %copy-start.8 = (f32[1,4096]{1,0:T(1,128)S(1)}, f32[1,4096]{1,0:T(1,128)}, u32[]{:S(2)}) copy-start(f32[1,4096]{1,0:T(1,128)} %gain_ref.3) | copy-start | bytes 49156
  28.9 2.6 %collective-permute-start.2 = (f32[2,128]{1,0:T(2,128)S(1)}, f32[2,128]{1,0:T(2,128)S(1)}, u32[]{:S(2)}, u32[]{:S(2)}) collective-permute-start(f32[2,128]{1,0:T(2,128)S(1)} %pad_maximum_fusion), channel_id=1, source_target_pairs={{0,1},{1,0},{2,3},{3,2},{4,5},{5,4},{6,7},{7,6},{8,9},{9,8},{10,11... | collective-permute-start | bytes 3080 | tf_op jit(solution)/shard_map/ppermute | solution.py:23
  31.5 0.6 copy-start.12
  44.3 2.7 %copy-start.1 = (f32[3,16,8,4096]{3,2,1,0:T(8,128)}, f32[3,16,8,4096]{3,2,1,0:T(8,128)S(1)}, u32[]{:S(2)}) copy-start(f32[3,16,8,4096]{3,2,1,0:T(8,128)S(1)} %get-tuple-element.11.e_ref) | copy-start | bytes 18874372
  47.0 0.7 copy-start.6
  87.9 2.8 %copy-start.2 = (f32[3,16,8,4096]{3,2,1,0:T(8,128)S(1)}, f32[3,16,8,4096]{3,2,1,0:T(8,128)}, u32[]{:S(2)}) copy-start(f32[3,16,8,4096]{3,2,1,0:T(8,128)} %copy-done.1) | copy-start | bytes 18874372
  90.7 1.4 %copy-start.4 = (bf16[12,16,4096]{2,1,0:T(8,128)(2,1)S(1)}, bf16[12,16,4096]{2,1,0:T(8,128)(2,1)}, u32[]{:S(2)}) copy-start(bf16[12,16,4096]{2,1,0:T(8,128)(2,1)} %all-gather.3.cloned.1.call-done) | copy-start | bytes 4718596
  92.1 0.9 copy-start.7
  93.1 0.7 copy-start.10
  115.2 1.3 %copy-start.3 = (f32[128,4096]{1,0:T(8,128)}, f32[128,4096]{1,0:T(8,128)S(1)}, u32[]{:S(2)}) copy-start(f32[128,4096]{1,0:T(8,128)S(1)} %get-tuple-element.14) | copy-start | bytes 6291460
  116.5 0.6 copy-start.9
  118.1 2.6 %collective-permute-start.3 = (f32[16,8]{1,0:T(8,128)S(1)}, f32[16,8]{1,0:T(8,128)S(1)}, u32[]{:S(2)}, u32[]{:S(2)}) collective-permute-start(f32[16,8]{1,0:T(8,128)S(1)} %reduce_sum.29), channel_id=1, source_target_pairs={{0,1},{1,0},{2,3},{3,2},{4,5},{5,4},{6,7},{7,6},{8,9},{9,8},{10,11... | collective-permute-start | bytes 1544 | tf_op jit(solution)/shard_map/ppermute | solution.py:23
Sparse Core Ops, SparseCore 0:
  47.9 40.0 all-gather.2

commit v2 on v1

--- a/solution.py
+++ b/solution.py
@@ -9,6 +9,7 @@
 ROWS = 8
 LANES = 128
 CHUNK = 512
+VMEM = 58 * 1024 * 1024
 epsilon = 1e-06
 
 
@@ -29,7 +30,34 @@
 
 
 def states_kernel(x_ref, sav_ref, cot_ref, sf_ref, sb_ref, gain_ref, decay_ref,
-                  e_ref, end_ref, sig, last):
+                  e_ref, recv_ref, sig, last, end_ref, send_sem, recv_sem):
+    peers = recv_ref.shape[0] + 1
+    mine = lax.axis_index("ctx")
+    chunk = x_ref.shape[1]
+    chunks = end_ref.shape[2] // chunk
+    step = pl.program_id(0)
+
+    def copy(c, far, rev):
+        lanes = pl.ds(pl.multiple_of(c * chunk, chunk), chunk)
+        parts = pl.ds(2, 1) if rev else pl.ds(0, 2)
+        index = 2 * (far - 1) + rev
+        return pltpu.make_async_remote_copy(
+            src_ref=end_ref.at[parts, :, lanes],
+            dst_ref=recv_ref.at[far - 1, parts, :, lanes],
+            send_sem=send_sem.at[c, index],
+            recv_sem=recv_sem.at[c, index],
+            device_id={"ctx": jnp.maximum(mine - far, 0) if rev else jnp.minimum(mine + far, peers - 1)},
+            device_id_type=pl.DeviceIdType.MESH,
+        )
+
+    @pl.when(step == 0)
+    def _():
+        barrier = pltpu.get_barrier_semaphore()
+        for far in range(1, peers):
+            pl.semaphore_signal(barrier, inc=1, device_id={"ctx": lax.rem(mine + far, peers)},
+                                device_id_type=pl.DeviceIdType.MESH)
+        pl.semaphore_wait(barrier, peers - 1)
+
     length = x_ref.shape[0]
     steps = length // ROWS
     modes = decay_ref.shape[0]
@@ -71,10 +99,37 @@
                 e_ref[q, k, :, lanes] = jnp.where(near, moved, 0.0)
                 edge = 0 if rev else ROWS - 1
                 last[k:k + 1, :] = total[edge:edge + 1, :]
-            end_ref[q, :, lanes] = last[...].astype(end_ref.dtype)
+            here = pl.ds(pl.multiple_of(step * chunk + g * LANES, LANES), LANES)
+            end_ref[q, :, here] = last[...].astype(end_ref.dtype)
         return carry
 
-    lax.fori_loop(0, x_ref.shape[1] // LANES, group, 0)
+    lax.fori_loop(0, chunk // LANES, group, 0)
+
+    for far in range(1, peers):
+        @pl.when(mine + far < peers)
+        def _():
+            copy(step, far, 0).start()
+
+        @pl.when(mine >= far)
+        def _():
+            copy(step, far, 1).start()
+
+    @pl.when(step == chunks - 1)
+    def _():
+        def finish(c, carry):
+            for far in range(1, peers):
+                @pl.when(mine + far < peers)
+                def _():
+                    copy(c, far, 0).wait_send()
+                    copy(c, far, 1).wait_recv()
+
+                @pl.when(mine >= far)
+                def _():
+                    copy(c, far, 1).wait_send()
+                    copy(c, far, 0).wait_recv()
+            return carry
+
+        lax.fori_loop(0, chunks, finish, 0)
 
 
 def finish_kernel(mine_ref, x_ref, sav_ref, cot_ref, sf_ref, sb_ref, gain_ref, skip_ref,
@@ -83,7 +138,7 @@
     length = x_ref.shape[0]
     steps = length // ROWS
     modes = decay_ref.shape[0]
-    peers = ends_ref.shape[0]
+    peers = ends_ref.shape[0] + 1
     mine = mine_ref[0]
     place = lax.broadcasted_iota(jnp.int32, (ROWS, LANES), 0).astype(jnp.float32)
 
@@ -105,10 +160,9 @@
         entering = []
         for q in range(3):
             total = jnp.zeros((modes, LANES), jnp.float32)
-            for hop in range(peers - 1):
-                at = peers - 1 - hop if q == 2 else hop
-                reached = (at > mine) if q == 2 else (at < mine)
-                longer = whole * total + ends_ref[at, q, :, lanes].astype(jnp.float32)
+            for far in range(peers - 1, 0, -1):
+                reached = (mine + far < peers) if q == 2 else (mine >= far)
+                longer = whole * total + ends_ref[far - 1, q, :, lanes].astype(jnp.float32)
                 total = jnp.where(reached, longer, total)
             entering.append(total)
         kernel = []
@@ -187,12 +241,19 @@
         jnp.bfloat16
     )
     embedded = jnp.dot(onehot, table, preferred_element_type=jnp.float32).astype(jnp.bfloat16)
+    sav = saved_in[0]
+
+    def squares_of(value):
+        value = value.astype(jnp.float32)
+        return jnp.sum(value * value, axis=1)
+
+    squares = width_sum(
+        jnp.stack([squares_of(boundary[0, 1]), squares_of(sav), squares_of(embedded)])
+    )
+    square_fwd = jnp.where(segment_index == 0, squares[2], shifted(squares[0], "pipe", 1))
     x = jnp.where(segment_index == 0, embedded, arrived)
     cot = jnp.where(segment_index == segments - 1, loss_grad, returned)
-    sav = saved_in[0]
-    x32, sav32 = x.astype(jnp.float32), sav.astype(jnp.float32)
-    squares = width_sum(jnp.stack([jnp.sum(x32 * x32, axis=1), jnp.sum(sav32 * sav32, axis=1)]))
-    scales = lax.rsqrt(squares / D + epsilon)
+    scales = lax.rsqrt(jnp.stack([square_fwd, squares[1]]) / D + epsilon)
     length, channels = x.shape
     modes = decay_rate.shape[1]
     steps = length // ROWS
@@ -205,23 +266,32 @@
     row = pl.BlockSpec((1, chunk), lambda c: (0, c))
     mode_spec = pl.BlockSpec((modes, chunk), lambda c: (0, c))
     e_spec = pl.BlockSpec((3, modes, ROWS, chunk), lambda c: (0, 0, 0, c))
-    params = pltpu.CompilerParams(vmem_limit_bytes=40 * 1024 * 1024)
+    params = pltpu.CompilerParams(vmem_limit_bytes=VMEM)
     f32 = jnp.float32
     work = length * channels
-    entries, ends = pl.pallas_call(
+    peers = lax.axis_size("ctx")
+    copies = (channels // chunk, 2 * (peers - 1))
+    entries, received = pl.pallas_call(
         states_kernel,
         grid=grid,
         in_specs=[tall, tall, tall, scale_spec, scale_spec, row, mode_spec],
-        out_specs=[e_spec, pl.BlockSpec((3, modes, chunk), lambda c: (0, 0, c))],
+        out_specs=[e_spec, pl.BlockSpec(memory_space=pl.ANY)],
         out_shape=[
             jax.ShapeDtypeStruct((3, modes, ROWS, channels), f32),
-            jax.ShapeDtypeStruct((3, modes, channels), jnp.bfloat16),
+            jax.ShapeDtypeStruct((peers - 1, 3, modes, channels), jnp.bfloat16),
         ],
-        scratch_shapes=[pltpu.VMEM((3, length, LANES), f32), pltpu.VMEM((modes, LANES), f32)],
-        compiler_params=params,
+        scratch_shapes=[
+            pltpu.VMEM((3, length, LANES), f32),
+            pltpu.VMEM((modes, LANES), f32),
+            pltpu.VMEM((3, modes, channels), jnp.bfloat16),
+            pltpu.SemaphoreType.DMA(copies),
+            pltpu.SemaphoreType.DMA(copies),
+        ],
+        compiler_params=pltpu.CompilerParams(
+            vmem_limit_bytes=VMEM, collective_id=0, has_side_effects=True
+        ),
         cost_estimate=pl.CostEstimate(flops=96 * work, bytes_accessed=18 * work, transcendentals=0),
     )(x, sav, cot, sf, sb, gain, decay_rate[0])
-    gathered = lax.all_gather(ends, "ctx")
     mine = lax.axis_index("ctx").astype(jnp.int32).reshape(1)
     out, part, gain_grad, skip_grad, inner = pl.pallas_call(
         finish_kernel,
@@ -229,7 +299,7 @@
         in_specs=[
             pl.BlockSpec(memory_space=pltpu.SMEM), tall, tall, tall, scale_spec, scale_spec,
             row, row, mode_spec, mode_spec, e_spec,
-            pl.BlockSpec((gathered.shape[0], 3, modes, chunk), lambda c: (0, 0, 0, c)),
+            pl.BlockSpec((peers - 1, 3, modes, chunk), lambda c: (0, 0, 0, c)),
         ],
         out_specs=[tall, tall, row, row, pl.BlockSpec((steps, ROWS, LANES), lambda c: (0, 0, 0))],
         out_shape=[
@@ -242,10 +312,10 @@
         scratch_shapes=[pltpu.VMEM((3, length, LANES), f32), pltpu.VMEM((3, length, LANES), f32)],
         compiler_params=params,
         cost_estimate=pl.CostEstimate(flops=150 * work, bytes_accessed=24 * work, transcendentals=0),
-    )(mine, x, sav, cot, sf, sb, gain, skip, residue[0], decay_rate[0], entries, gathered)
+    )(mine, x, sav, cot, sf, sb, gain, skip, residue[0], decay_rate[0], entries, received)
     inner_sum = width_sum(jnp.sum(inner, axis=2)).T.reshape(length)
     factor = (scales[1] ** 2 * inner_sum / D)[:, None]
-    input_grad = (part - sav32 * factor).astype(jnp.bfloat16)
+    input_grad = (part - sav.astype(f32) * factor).astype(jnp.bfloat16)
     return (out[None], input_grad[None], gain_grad[None], skip_grad[None])
 
 

time: 134 us -> 94.9 us (0.71)
  the two profiles are of different devices: /device:TPU:1 before, /device:TPU:30 now
where the time goes in v2:
time: 94.9 us; the launch traced here: 94.5 us
  Pallas kernels  51.9 us (55%)
  waiting for transfers between devices  17 us (18%)
  starting transfers between devices  8.8 us (9%)
  other arithmetic  7.03 us (7%)
  local copies, waits for them, and re-layouts  4.83 us (5%)
  matrix products  4.21 us (4%)
    pallas_call x1, Pallas kernels, local(): pl.pallas_call(states_kernel, grid=grid, in_specs=[tall, tall, tall, scal...  29.3 us
    pallas_call x1, Pallas kernels, local(): pl.pallas_call(finish_kernel, grid=grid, in_specs=[pl.BlockSpec(memory_sp...  22.6 us
    ppermute x3, waiting for transfers between devices, shifted(): lax.ppermute(value, axis, [(source, source + steps) for source in range(i...  10.8 us
    ppermute x3, starting transfers between devices, shifted(): lax.ppermute(value, axis, [(source, source + steps) for source in range(i...  7.61 us
    ppermute x2, waiting for transfers between devices, width_sum(): return value + lax.ppermute(value, 'width', [(0, 1), (1, 0)])  6.17 us
    dot_general x1, matrix products, local(): jnp.dot(onehot, table, preferred_element_type=jnp.float32)  4.21 us
    squeeze x1, local copies, waits for them, and re-layouts, local(): returned = shifted(boundary[0, 0], 'pipe', -1)  3.23 us
    broadcast_in_dim x1, other arithmetic, local(): return (out[None], input_grad[None], gain_grad[None], skip_grad[None])  2.89 us
  transfers between devices with their start and end apart: 5, of which 4 were waited for; matrix products, arithmetic and copies ran while one was open for 8% of the time, Pallas kernels for 0%

profile of v2, /device:TPU:30, one launch (start us, length us, event | category | flops | bytes accessed | tf_op | source)
XLA Modules:
  0.0 94.5 jit_solution(12405824603313706841)
XLA Ops:
  0.6 0.0 copy-start.2
  0.6 0.0 copy-start
  0.7 3.2 %slice_bitcast_fusion = (bf16[128,4096]{1,0:T(8,128)(2,1)}, bf16[128,4096]{1,0:T(8,128)(2,1)}) fusion(bf16[1,2,128,4096]{3,2,1,0:T(8,128)(2,1)} %param.11), kind=kLoop, calls=%fused_computation.9 | loop fusion | bytes 4194304 | tf_op jit(solution)/shard_map/squeeze | solution.py:239
  3.9 0.0 copy-start.4
  3.9 2.0 %collective-permute-start = (bf16[128,4096]{1,0:T(8,128)(2,1)}, bf16[128,4096]{1,0:T(8,128)(2,1)}, u32[]{:S(2)}, u32[]{:S(2)}) collective-permute-start(bf16[128,4096]{1,0:T(8,128)(2,1)} %get-tuple-element.19), channel_id=1, source_target_pairs={{0,8},{8,16},{16,24},{1,9},{9,17},{17,25},{2,10},{10,18},{18,26},{... | collective-permute-start | bytes 3145736 | tf_op jit(solution)/shard_map/ppermute | solution.py:19
  5.9 3.6 %collective-permute-start.1 = (bf16[128,4096]{1,0:T(8,128)(2,1)}, bf16[128,4096]{1,0:T(8,128)(2,1)}, u32[]{:S(2)}, u32[]{:S(2)}) collective-permute-start(bf16[128,4096]{1,0:T(8,128)(2,1)} %get-tuple-element.18), channel_id=1, source_target_pairs={{8,0},{16,8},{24,16},{9,1},{17,9},{25,17},{10,2},{18,10},{26,18},{... | collective-permute-start | bytes 3145736 | tf_op jit(solution)/shard_map/ppermute | solution.py:19
  9.6 0.0 copy-done
  9.6 0.3 fusion
  9.9 0.0 copy-done.2
  9.9 0.3 multiply_reduce_fusion.1
  10.2 0.0 copy-start.3
  10.2 10.2 %collective-permute-done = bf16[128,4096]{1,0:T(8,128)(2,1)} collective-permute-done((bf16[128,4096]{1,0:T(8,128)(2,1)}, bf16[128,4096]{1,0:T(8,128)(2,1)}, u32[]{:S(2)}, u32[]{:S(2)}) %collective-permute-start) | collective-permute-done | bytes 1048608 | tf_op jit(solution)/shard_map/ppermute | solution.py:19
  20.4 0.0 copy-done.4
  20.4 4.2 %broadcast_select_fusion.1 = (bf16[128,4096]{1,0:T(8,128)(2,1)}, bf16[128,4096]{1,0:T(8,128)(2,1)S(1)}) fusion(bf16[128,4096]{1,0:T(8,128)(2,1)} %collective-permute-done, pred[]{:T(512)S(6)} %eq.20, bf16[512,4096]{1,0:T(8,128)(2,1)} %param.10, s32[128]{0:T(128)S(1)} %copy-done.4), kind=kOutput, calls=%fused_computation.12 | convolution fusion | flops 537985024 | bytes 7340545 | tf_op jit(solution)/shard_map/dot_general | solution.py:243
  24.7 0.3 multiply_reduce_fusion
  25.0 0.6 collective-permute-start.2
  25.6 3.1 %collective-permute-done.2 = f32[3,128]{1,0:T(4,128)S(1)} collective-permute-done((f32[3,128]{1,0:T(4,128)S(1)}, f32[3,128]{1,0:T(4,128)S(1)}, u32[]{:S(2)}, u32[]{:S(2)}) %collective-permute-start.2) | collective-permute-done | bytes 1568 | tf_op jit(solution)/shard_map/ppermute | solution.py:24
  28.6 1.9 %collective-permute-start.3 = (f32[128]{0:T(128)S(1)}, f32[128]{0:T(128)S(1)}, u32[]{:S(2)}, u32[]{:S(2)}) collective-permute-start(f32[128]{0:T(128)S(1)} %get-tuple-element.20), channel_id=1, source_target_pairs={{0,8},{8,16},{16,24},{1,9},{9,17},{17,25},{2,10},{10,18},{18,26},{... | collective-permute-start | bytes 1544 | tf_op jit(solution)/shard_map/ppermute | solution.py:19
  30.6 0.0 collective-permute-done.1
  30.6 0.0 copy-done.3
  30.6 2.3 %broadcast_select_fusion.cot_ref = bf16[128,4096]{1,0:T(8,128)(2,1)} fusion(bf16[128,4096]{1,0:T(8,128)(2,1)S(1)} %copy-done.3, bf16[128,4096]{1,0:T(8,128)(2,1)} %collective-permute-done.1, pred[]{:T(512)S(6)} %eq.24), kind=kLoop, calls=%fused_computation.11 | loop fusion | flops 524288 | bytes 3145729 | tf_op jit(solution)/shard_map/jit(_where)/select_n | solution.py:255
  32.9 0.6 collective-permute-done.3
  33.5 0.7 broadcast_in_dim.32.sb_ref
  34.2 0.7 broadcast_in_dim.30.sf_ref
  34.9 29.3 %shard_map.120 = (f32[3,16,8,4096]{3,2,1,0:T(8,128)}, bf16[3,3,16,4096]{3,2,1,0:T(8,128)(2,1)}) custom-call(bf16[128,4096]{1,0:T(8,128)(2,1)} %get-tuple-element.24.x_ref, bf16[128,4096]{1,0:T(8,128)(2,1)} %bitcast.35, bf16[128,4096]{1,0:T(8,128)(2,1)} %broadcast_select_fusion.cot_ref, f32[128,128]{1,0:T(8,128)} %broadcast_in_dim.30.sf_ref, ...), custom_call_target="tpu_custom_call" | custom-call | flops 50331648 | bytes 9437184 | tf_op jit(solution)/shard_map/pallas_call | solution.py:274
  64.2 0.0 copy-start.1
  64.2 22.6 %shard_map.121 = (bf16[128,4096]{1,0:T(8,128)(2,1)}, f32[128,4096]{1,0:T(8,128)}, f32[1,4096]{1,0:T(1,128)}, f32[1,4096]{1,0:T(1,128)}, f32[16,8,128]{2,1,0:T(8,128)}) custom-call(s32[1]{0:T(128)} %bitcast.mine_ref, bf16[128,4096]{1,0:T(8,128)(2,1)} %get-tuple-element.24.x_ref, bf16[128,4096]{1,0:T(8,128)(2,1)} %bitcast.36, ...), custom_call_target="tpu_custom_call" | custom-call | flops 78643200 | bytes 12582912 | tf_op jit(solution)/shard_map/pallas_call | solution.py:296
  86.8 0.9 reduce_sum.39
  87.8 0.6 collective-permute-start.4
  88.4 3.1 %collective-permute-done.4 = f32[16,8]{1,0:T(8,128)S(1)} collective-permute-done((f32[16,8]{1,0:T(8,128)S(1)}, f32[16,8]{1,0:T(8,128)S(1)}, u32[]{:S(2)}, u32[]{:S(2)}) %collective-permute-start.4) | collective-permute-done | bytes 544 | tf_op jit(solution)/shard_map/ppermute | solution.py:24
  91.5 0.1 copy.13
  91.6 0.1 reshape.29
  91.7 0.0 copy-done.1
  91.7 2.9 %fusion.3 = bf16[1,128,4096]{2,1,0:T(8,128)(2,1)} fusion(f32[128,4096]{1,0:T(8,128)} %get-tuple-element.14, f32[128]{0:T(128)S(1)} %multiply_multiply_fusion, bf16[1,128,4096]{2,1,0:T(8,128)(2,1)S(1)} %copy-done.1), kind=kLoop, calls=%fused_computation.8 | loop fusion | flops 2097152 | bytes 4194816 | tf_op jit(solution)/shard_map/broadcast_in_dim | solution.py:319
  (8 shorter events, 0.1 us)
Async XLA Ops:
  0.6 9.3 %copy-start.2 = (bf16[1,2,128,4096]{3,2,1,0:T(8,128)(2,1)S(1)}, bf16[1,2,128,4096]{3,2,1,0:T(8,128)(2,1)}, u32[]{:S(2)}) copy-start(bf16[1,2,128,4096]{3,2,1,0:T(8,128)(2,1)} %param.11) | copy-start | bytes 6291460
  0.6 9.0 %copy-start = (bf16[1,128,4096]{2,1,0:T(8,128)(2,1)S(1)}, bf16[1,128,4096]{2,1,0:T(8,128)(2,1)}, u32[]{:S(2)}) copy-start(bf16[1,128,4096]{2,1,0:T(8,128)(2,1)} %param.12) | copy-start | bytes 3145732
  3.9 16.6 %copy-start.4 = (s32[128]{0:T(128)S(1)}, s32[128]{0:T(128)}, u32[]{:S(2)}) copy-start(s32[128]{0:T(128)} %param.9) | copy-start | bytes 1540
  3.9 16.6 %collective-permute-start = (bf16[128,4096]{1,0:T(8,128)(2,1)}, bf16[128,4096]{1,0:T(8,128)(2,1)}, u32[]{:S(2)}, u32[]{:S(2)}) collective-permute-start(bf16[128,4096]{1,0:T(8,128)(2,1)} %get-tuple-element.19), channel_id=1, source_target_pairs={{0,8},{8,16},{16,24},{1,9},{9,17},{17,25},{2,10},{10,18},{18,26},{... | collective-permute-start | bytes 3145736 | tf_op jit(solution)/shard_map/ppermute | solution.py:19
  5.9 24.6 %collective-permute-start.1 = (bf16[128,4096]{1,0:T(8,128)(2,1)}, bf16[128,4096]{1,0:T(8,128)(2,1)}, u32[]{:S(2)}, u32[]{:S(2)}) collective-permute-start(bf16[128,4096]{1,0:T(8,128)(2,1)} %get-tuple-element.18), channel_id=1, source_target_pairs={{8,0},{16,8},{24,16},{9,1},{17,9},{25,17},{10,2},{18,10},{26,18},{... | collective-permute-start | bytes 3145736 | tf_op jit(solution)/shard_map/ppermute | solution.py:19
  10.2 20.4 %copy-start.3 = (bf16[128,4096]{1,0:T(8,128)(2,1)S(1)}, bf16[128,4096]{1,0:T(8,128)(2,1)}, u32[]{:S(2)}) copy-start(bf16[128,4096]{1,0:T(8,128)(2,1)} %param.13) | copy-start | bytes 3145732
  25.0 3.7 %collective-permute-start.2 = (f32[3,128]{1,0:T(4,128)S(1)}, f32[3,128]{1,0:T(4,128)S(1)}, u32[]{:S(2)}, u32[]{:S(2)}) collective-permute-start(f32[3,128]{1,0:T(4,128)S(1)} %pad_maximum_fusion), channel_id=1, source_target_pairs={{0,1},{1,0},{2,3},{3,2},{4,5},{5,4},{6,7},{7,6},{8,9},{9,8},{10,11... | collective-permute-start | bytes 4616 | tf_op jit(solution)/shard_map/ppermute | solution.py:24
  28.6 4.9 %collective-permute-start.3 = (f32[128]{0:T(128)S(1)}, f32[128]{0:T(128)S(1)}, u32[]{:S(2)}, u32[]{:S(2)}) collective-permute-start(f32[128]{0:T(128)S(1)} %get-tuple-element.20), channel_id=1, source_target_pairs={{0,8},{8,16},{16,24},{1,9},{9,17},{17,25},{2,10},{10,18},{18,26},{... | collective-permute-start | bytes 1544 | tf_op jit(solution)/shard_map/ppermute | solution.py:19
  64.2 27.5 %copy-start.1 = (bf16[1,128,4096]{2,1,0:T(8,128)(2,1)S(1)}, bf16[1,128,4096]{2,1,0:T(8,128)(2,1)}, u32[]{:S(2)}) copy-start(bf16[1,128,4096]{2,1,0:T(8,128)(2,1)} %param.12) | copy-start | bytes 3145732
  87.8 3.7 %collective-permute-start.4 = (f32[16,8]{1,0:T(8,128)S(1)}, f32[16,8]{1,0:T(8,128)S(1)}, u32[]{:S(2)}, u32[]{:S(2)}) collective-permute-start(f32[16,8]{1,0:T(8,128)S(1)} %reduce_sum.39), channel_id=1, source_target_pairs={{0,1},{1,0},{2,3},{3,2},{4,5},{5,4},{6,7},{7,6},{8,9},{9,8},{10,11... | collective-permute-start | bytes 1544 | tf_op jit(solution)/shard_map/ppermute | solution.py:24

commit v3 on v0

v3 whole, which is shorter than its diff:
```python
import functools

import jax
import jax.numpy as jnp
from jax import lax
from jax.experimental import pallas as pl
from jax.experimental.pallas import tpu as pltpu
from jax.sharding import PartitionSpec as P

D = 8192
ROWS = 8
LANES = 128
CHUNK = 512
VMEM = 58 * 1024 * 1024
epsilon = 1e-06


def shifted(value, axis, steps):
    count = lax.axis_size(axis)
    initial, last = (max(0, -steps), min(count, count - steps))
    return lax.ppermute(value, axis, [(source, source + steps) for source in range(initial, last)])


def width_sum(value):
    if lax.axis_size("width") == 2:
        return value + lax.ppermute(value, "width", [(0, 1), (1, 0)])
    return lax.psum(value, "width")


def wide(row):
    return jnp.broadcast_to(row, (ROWS, LANES))


def step_kernel(segments, emb_ref, arr_ref, sav_ref, loss_ref, ret_ref, scale_ref, gain_ref,
                decay_ref, skip_ref, residue_ref,
                out_ref, part_ref, gg_ref, sg_ref, acc_ref,
                sig, res, last, e_all, end_ref, recv_ref, send_sem, recv_sem):
    peers = recv_ref.shape[0] + 1
    mine = lax.axis_index("ctx")
    segment = lax.axis_index("pipe")
    chunk = sav_ref.shape[1]
    chunks = end_ref.shape[2] // chunk
    step = pl.program_id(0)
    sf_ref, sb_ref = scale_ref.at[0], scale_ref.at[1]
    length = sav_ref.shape[0]
    steps = length // ROWS
    modes = decay_ref.shape[0]

    def incoming(lanes):
        return jnp.where(segment == 0, emb_ref[:, lanes].astype(jnp.float32),
                         arr_ref[:, lanes].astype(jnp.float32))

    def cotangent(lanes):
        return jnp.where(segment == segments - 1, loss_ref[:, lanes].astype(jnp.float32),
                         ret_ref[:, lanes].astype(jnp.float32))

    def copy(c, far, rev):
        lanes = pl.ds(pl.multiple_of(c * chunk, chunk), chunk)
        parts = pl.ds(2, 1) if rev else pl.ds(0, 2)
        index = 2 * (far - 1) + rev
        return pltpu.make_async_remote_copy(
            src_ref=end_ref.at[parts, :, lanes],
            dst_ref=recv_ref.at[far - 1, parts, :, lanes],
            send_sem=send_sem.at[c, index],
            recv_sem=recv_sem.at[c, index],
            device_id={"ctx": jnp.maximum(mine - far, 0) if rev else jnp.minimum(mine + far, peers - 1)},
            device_id_type=pl.DeviceIdType.MESH,
        )

    @pl.when(step == 0)
    def _():
        barrier = pltpu.get_barrier_semaphore()
        for far in range(1, peers):
            pl.semaphore_signal(barrier, inc=1, device_id={"ctx": lax.rem(mine + far, peers)},
                                device_id_type=pl.DeviceIdType.MESH)
        pl.semaphore_wait(barrier, peers - 1)
        acc_ref[...] = jnp.zeros_like(acc_ref)

    @pl.when(step < chunks)
    def _():
        place = lax.broadcasted_iota(jnp.int32, (ROWS, LANES), 0)

        def group(g, carry):
            lanes = pl.ds(pl.multiple_of(g * LANES, LANES), LANES)
            gain = gain_ref[:, lanes]
            back = sav_ref[:, lanes].astype(jnp.float32) * sb_ref[...] * gain
            sig[0] = incoming(lanes) * sf_ref[...] * gain
            sig[1] = back
            sig[2] = cotangent(lanes) * back
            damping = decay_ref[:, lanes]
            here = pl.ds(pl.multiple_of(step * chunk + g * LANES, LANES), LANES)
            a_all = jnp.exp(-damping)
            stride_all = jnp.exp(-damping * float(steps))
            a = [wide(a_all[k:k + 1]) for k in range(modes)]
            for q in range(3):
                rev = q == 2
                order = range(steps - 1, -1, -1) if rev else range(steps)
                state = None
                for j in order:
                    piece = sig[q, pl.ds(j, ROWS, stride=steps), :]
                    if state is None:
                        state = [piece] * modes
                    else:
                        state = [a[k] * state[k] + piece for k in range(modes)]
                for k in range(modes):
                    power = wide(stride_all[k:k + 1])
                    total = state[k]
                    hop = 1
                    while hop < ROWS:
                        near = (place < ROWS - hop) if rev else (place >= hop)
                        moved = pltpu.roll(total, ROWS - hop if rev else hop, 0)
                        total = total + jnp.where(near, power * moved, 0.0)
                        power = power * power
                        hop *= 2
                    near = (place < ROWS - 1) if rev else (place >= 1)
                    moved = pltpu.roll(total, ROWS - 1 if rev else 1, 0)
                    e_all[q, k, :, here] = jnp.where(near, moved, 0.0)
                    edge = 0 if rev else ROWS - 1
                    last[k:k + 1, :] = total[edge:edge + 1, :]
                end_ref[q, :, here] = last[...].astype(end_ref.dtype)
            return carry

        lax.fori_loop(0, chunk // LANES, group, 0)

        for far in range(1, peers):
            @pl.when(mine + far < peers)
            def _():
                copy(step, far, 0).start()

            @pl.when(mine >= far)
            def _():
                copy(step, far, 1).start()

    @pl.when(step >= chunks)
    def _():
        place = lax.broadcasted_iota(jnp.int32, (ROWS, LANES), 0).astype(jnp.float32)

        c = step - chunks
        for far in range(1, peers):
            @pl.when(mine + far < peers)
            def _():
                copy(c, far, 0).wait_send()
                copy(c, far, 1).wait_recv()

            @pl.when(mine >= far)
            def _():
                copy(c, far, 1).wait_send()
                copy(c, far, 0).wait_recv()

        def group(g, carry):
            lanes = pl.ds(pl.multiple_of(g * LANES, LANES), LANES)
            gain = gain_ref[:, lanes]
            gain_w = wide(gain)
            sig[0] = incoming(lanes)
            sig[1] = sav_ref[:, lanes].astype(jnp.float32) * sb_ref[...]
            sig[2] = cotangent(lanes)
            damping = decay_ref[:, lanes]
            a_all = jnp.exp(-damping)
            coefs = residue_ref[:, lanes] * jnp.sqrt(1.0 - jnp.exp(-2.0 * damping))
            here = pl.ds(pl.multiple_of(c * chunk + g * LANES, LANES), LANES)
            whole = jnp.exp(-damping * float(length))
            entering = []
            for q in range(3):
                total = jnp.zeros((modes, LANES), jnp.float32)
                for far in range(peers - 1, 0, -1):
                    reached = (mine + far < peers) if q == 2 else (mine >= far)
                    longer = whole * total + recv_ref[far - 1, q, :, here].astype(jnp.float32)
                    total = jnp.where(reached, longer, total)
                entering.append(total)
            kernel = []
            power = coefs
            for n in range(steps):
                kernel.append(wide(jnp.sum(power, axis=0, keepdims=True)))
                power = power * a_all
            kernel[0] = kernel[0] + wide(skip_ref[:, lanes])

            def rows(i):
                return pl.ds(i, ROWS, stride=steps)

            def conv(q, pieces, emit):
                rev = q == 2
                ago = (float(ROWS - 1) - place) if rev else place
                decayed = []
                for k in range(modes):
                    gap = jnp.exp(wide(damping[k:k + 1]) * (ago * float(-steps)))
                    state = e_all[q, k, :, here] + gap * wide(entering[q][k:k + 1])
                    decayed.append(wide(coefs[k:k + 1]) * state)
                a = [wide(a_all[k:k + 1]) for k in range(modes)]
                for n in range(steps):
                    decayed = [a[k] * decayed[k] for k in range(modes)]
                    terms = decayed + [kernel[n - m] * pieces[steps - 1 - m if rev else m]
                                       for m in range(n + 1)]
                    sums = terms[:4]
                    for index, term in enumerate(terms[4:]):
                        sums[index % 4] = sums[index % 4] + term
                    emit(steps - 1 - n if rev else n, (sums[0] + sums[1]) + (sums[2] + sums[3]))

            raw = [sig[0, rows(i), :] for i in range(steps)]
            normed = [raw[i] * sf_ref[rows(i), :] * gain_w for i in range(steps)]

            def emit_out(i, value):
                res[0, rows(i), :] = sig[0, rows(i), :] + sig[0, rows(i), :] * sf_ref[rows(i), :] * gain_w * value

            conv(0, normed, emit_out)
            out_ref[:, lanes] = res[0].astype(out_ref.dtype)

            back = [sig[1, rows(i), :] * gain_w for i in range(steps)]

            def emit_mixed(i, value):
                res[1, rows(i), :] = sig[2, rows(i), :] * value

            conv(1, back, emit_mixed)

            mix = [sig[2, rows(i), :] * back[i] for i in range(steps)]
            skip_sum = mix[0] * back[0]
            for i in range(1, steps):
                skip_sum = skip_sum + mix[i] * back[i]
            sg_ref[:, lanes] = jnp.sum(skip_sum, axis=0, keepdims=True)
            gain_sums = [jnp.zeros((ROWS, LANES), jnp.float32)]

            def emit_grad(i, value):
                norm = res[1, rows(i), :] + value
                unit = sig[1, rows(i), :]
                gain_sums[0] = gain_sums[0] + norm * unit
                scaled = gain_w * norm
                acc_ref[i] = acc_ref[i] + scaled * unit
                res[2, rows(i), :] = sig[2, rows(i), :] + sb_ref[rows(i), :] * scaled

            conv(2, mix, emit_grad)
            part_ref[:, lanes] = res[2]
            gg_ref[:, lanes] = jnp.sum(gain_sums[0], axis=0, keepdims=True)
            return carry

        lax.fori_loop(0, chunk // LANES, group, 0)


def local(tokens, table, boundary, saved_in, loss_grad, gain, skip, residue, decay_rate):
    segment_index = lax.axis_index("pipe")
    segments = lax.axis_size("pipe")
    arrived = shifted(boundary[0, 1], "pipe", 1)
    returned = shifted(boundary[0, 0], "pipe", -1)
    onehot = (tokens[:, None] == jnp.arange(table.shape[0], dtype=jnp.int32)[None, :]).astype(
        jnp.bfloat16
    )
    embedded = jnp.dot(onehot, table, preferred_element_type=jnp.float32).astype(jnp.bfloat16)
    sav = saved_in[0]

    def squares_of(value):
        value = value.astype(jnp.float32)
        return jnp.sum(value * value, axis=1)

    squares = width_sum(
        jnp.stack([squares_of(boundary[0, 1]), squares_of(sav), squares_of(embedded)])
    )
    square_fwd = jnp.where(segment_index == 0, squares[2], shifted(squares[0], "pipe", 1))
    scales = lax.rsqrt(jnp.stack([square_fwd, squares[1]]) / D + epsilon)
    length, channels = sav.shape
    modes = decay_rate.shape[1]
    steps = length // ROWS
    scale_tiles = jnp.broadcast_to(scales[:, :, None], (2, length, LANES))
    chunk = min(CHUNK, channels)
    chunks = channels // chunk
    peers = lax.axis_size("ctx")
    f32 = jnp.float32
    work = length * channels

    def both(height):
        return pl.BlockSpec((height, chunk), lambda s: (0, lax.rem(s, chunks)))

    def late(height):
        return pl.BlockSpec((height, chunk), lambda s: (0, jnp.maximum(s - chunks, 0)))

    out, part, gain_grad, skip_grad, inner = pl.pallas_call(
        functools.partial(step_kernel, segments),
        grid=(2 * chunks,),
        in_specs=[
            both(length), both(length), both(length), both(length), both(length),
            pl.BlockSpec((2, length, LANES), lambda s: (0, 0, 0)),
            both(1), both(modes), late(1), late(modes),
        ],
        out_specs=[late(length), late(length), late(1), late(1),
                   pl.BlockSpec((steps, ROWS, LANES), lambda s: (0, 0, 0))],
        out_shape=[
            jax.ShapeDtypeStruct((length, channels), jnp.bfloat16),
            jax.ShapeDtypeStruct((length, channels), f32),
            jax.ShapeDtypeStruct((1, channels), f32),
            jax.ShapeDtypeStruct((1, channels), f32),
            jax.ShapeDtypeStruct((steps, ROWS, LANES), f32),
        ],
        scratch_shapes=[
            pltpu.VMEM((3, length, LANES), f32),
            pltpu.VMEM((3, length, LANES), f32),
            pltpu.VMEM((modes, LANES), f32),
            pltpu.VMEM((3, modes, ROWS, channels), f32),
            pltpu.VMEM((3, modes, channels), jnp.bfloat16),
            pltpu.VMEM((peers - 1, 3, modes, channels), jnp.bfloat16),
            pltpu.SemaphoreType.DMA((chunks, 2 * (peers - 1))),
            pltpu.SemaphoreType.DMA((chunks, 2 * (peers - 1))),
        ],
        compiler_params=pltpu.CompilerParams(
            vmem_limit_bytes=VMEM, collective_id=0, has_side_effects=True
        ),
        cost_estimate=pl.CostEstimate(flops=246 * work, bytes_accessed=26 * work, transcendentals=0),
    )(embedded, arrived, sav, loss_grad, returned, scale_tiles, gain, decay_rate[0], skip, residue[0])
    inner_sum = width_sum(jnp.sum(inner, axis=2)).T.reshape(length)
    factor = (scales[1] ** 2 * inner_sum / D)[:, None]
    input_grad = (part - sav.astype(f32) * factor).astype(jnp.bfloat16)
    return (out[None], input_grad[None], gain_grad[None], skip_grad[None])


def solution(mesh):
    in_specs = (
        P("ctx"),
        P(None, "width"),
        P("pipe", None, "ctx", "width"),
        P("pipe", "ctx", "width"),
        P("ctx", "width"),
        P("pipe", "width"),
        P("pipe", "width"),
        P("pipe", None, "width"),
        P("pipe", None, "width"),
    )
    out_specs = (
        P("pipe", "ctx", "width"),
        P("pipe", "ctx", "width"),
        P("pipe", "ctx", "width"),
        P("pipe", "ctx", "width"),
    )
    return jax.shard_map(local, mesh=mesh, in_specs=in_specs, out_specs=out_specs, check_vma=False)
```

time: 1070 us -> 74.7 us (0.07)
  the two profiles are of different devices: /device:TPU:6 before, /device:TPU:1 now
where the time goes in v3:
time: 74.7 us; the launch traced here: 73.2 us
  Pallas kernels  40.6 us (54%)
  starting transfers between devices  12.6 us (17%)
  local copies, waits for them, and re-layouts  6.92 us (9%)
  other arithmetic  4.52 us (6%)
  matrix products  4.04 us (5%)
  waiting for transfers between devices  3.74 us (5%)
  between operations  0.78 us (1%)
    pallas_call x1, Pallas kernels, local(): pl.pallas_call(functools.partial(step_kernel, segments), grid=(2 * chunks...  40.6 us
    ppermute x3, starting transfers between devices, shifted(): lax.ppermute(value, axis, [(source, source + steps) for source in range(i...  10.1 us
    dot_general x1, matrix products, local(): jnp.dot(onehot, table, preferred_element_type=jnp.float32)  4.04 us
    squeeze x1, local copies, waits for them, and re-layouts, local(): returned = shifted(boundary[0, 0], 'pipe', -1)  3.22 us
    broadcast_in_dim x1, other arithmetic, local(): return (out[None], input_grad[None], gain_grad[None], skip_grad[None])  2.98 us
    unnamed x21, local copies, waits for them, and re-layouts  2.65 us
    ppermute x2, starting transfers between devices, width_sum(): return value + lax.ppermute(value, 'width', [(0, 1), (1, 0)])  2.55 us
    ppermute x2, waiting for transfers between devices, width_sum(): return value + lax.ppermute(value, 'width', [(0, 1), (1, 0)])  2.51 us
  transfers between devices with their start and end apart: 5, of which 3 were waited for; matrix products, arithmetic and copies ran while one was open for 6% of the time, Pallas kernels for 0%

profile of v3, /device:TPU:1, one launch (start us, length us, event | category | flops | bytes accessed | tf_op | source)
XLA Modules:
  0.0 73.2 jit_solution(497013930072432865)
XLA Ops:
  0.6 0.0 copy-start.2
  0.6 0.0 copy-start.8
  0.7 3.2 %slice_bitcast_fusion = (bf16[128,4096]{1,0:T(8,128)(2,1)}, bf16[128,4096]{1,0:T(8,128)(2,1)}) fusion(bf16[1,2,128,4096]{3,2,1,0:T(8,128)(2,1)} %param.11), kind=kLoop, calls=%fused_computation.9 | loop fusion | bytes 4194304 | tf_op jit(solution)/shard_map/squeeze | solution.py:241
  3.9 2.0 %collective-permute-start.1 = (bf16[128,4096]{1,0:T(8,128)(2,1)}, bf16[128,4096]{1,0:T(8,128)(2,1)S(1)}, u32[]{:S(2)}, u32[]{:S(2)}) collective-permute-start(bf16[128,4096]{1,0:T(8,128)(2,1)} %get-tuple-element.14), channel_id=1, source_target_pairs={{8,0},{16,8},{24,16},{9,1},{17,9},{25,17},{10,2},{18,10},{26,18},{... | collective-permute-start | bytes 3145736 | tf_op jit(solution)/shard_map/ppermute | solution.py:21
  5.8 4.5 %collective-permute-start = (bf16[128,4096]{1,0:T(8,128)(2,1)}, bf16[128,4096]{1,0:T(8,128)(2,1)S(1)}, u32[]{:S(2)}, u32[]{:S(2)}) collective-permute-start(bf16[128,4096]{1,0:T(8,128)(2,1)} %get-tuple-element.15), channel_id=1, source_target_pairs={{0,8},{8,16},{16,24},{1,9},{9,17},{17,25},{2,10},{10,18},{18,26},{... | collective-permute-start | bytes 3145736 | tf_op jit(solution)/shard_map/ppermute | solution.py:21
  10.3 0.0 copy-done.2
  10.3 0.3 multiply_reduce_fusion.1
  10.6 0.0 copy-done.8
  10.6 0.0 copy-start
  10.7 4.0 %multiply_reduce_fusion = (f32[128]{0:T(128)S(1)}, bf16[128,4096]{1,0:T(8,128)(2,1)}) fusion(bf16[512,4096]{1,0:T(8,128)(2,1)} %param.10, s32[128]{0:T(128)S(1)} %copy-done.8), kind=kOutput, calls=%fused_computation.6 | convolution fusion | flops 539033472 | bytes 5243904 | tf_op jit(solution)/shard_map/dot_general | solution.py:245
  14.7 0.0 copy-done
  14.7 0.3 fusion
  15.0 1.3 %collective-permute-start.2 = (f32[3,128]{1,0:T(4,128)S(1)}, f32[3,128]{1,0:T(4,128)S(1)}, u32[]{:S(2)}, u32[]{:S(2)}) collective-permute-start(f32[3,128]{1,0:T(4,128)S(1)} %pad_maximum_fusion), channel_id=1, source_target_pairs={{0,1},{1,0},{2,3},{3,2},{4,5},{5,4},{6,7},{7,6},{8,9},{9,8},{10,11... | collective-permute-start | bytes 4616 | tf_op jit(solution)/shard_map/ppermute | solution.py:26
  16.3 1.2 %collective-permute-done.2 = f32[3,128]{1,0:T(4,128)S(1)} collective-permute-done((f32[3,128]{1,0:T(4,128)S(1)}, f32[3,128]{1,0:T(4,128)S(1)}, u32[]{:S(2)}, u32[]{:S(2)}) %collective-permute-start.2) | collective-permute-done | bytes 1568 | tf_op jit(solution)/shard_map/ppermute | solution.py:26
  17.5 3.6 %collective-permute-start.3 = (f32[128]{0:T(128)S(1)}, f32[128]{0:T(128)S(1)}, u32[]{:S(2)}, u32[]{:S(2)}) collective-permute-start(f32[128]{0:T(128)S(1)} %get-tuple-element.16), channel_id=1, source_target_pairs={{0,8},{8,16},{16,24},{1,9},{9,17},{17,25},{2,10},{10,18},{18,26},{... | collective-permute-start | bytes 1544 | tf_op jit(solution)/shard_map/ppermute | solution.py:21
  21.1 1.2 %collective-permute-done.3 = f32[128]{0:T(128)S(1)} collective-permute-done((f32[128]{0:T(128)S(1)}, f32[128]{0:T(128)S(1)}, u32[]{:S(2)}, u32[]{:S(2)}) %collective-permute-start.3) | collective-permute-done | bytes 544 | tf_op jit(solution)/shard_map/ppermute | solution.py:21
  22.4 0.0 collective-permute-done.1.ret_ref
  22.4 0.0 copy-start.4
  22.4 0.0 collective-permute-done.arr_ref
  22.4 0.0 copy-start.5
  22.4 0.9 %broadcast_in_dim.10.scale_ref = f32[2,128,128]{2,1,0:T(8,128)} broadcast(f32[2,128]{1,0:T(2,128)S(1)} %fusion.6), dimensions={0,1} | broadcast | bytes 132096 | tf_op jit(solution)/shard_map/broadcast_in_dim | solution.py:260
  23.3 0.1 copy-done.4
  23.4 0.3 copy-done.5
  23.8 0.0 copy-start.1
  23.8 40.6 %shard_map.120 = (bf16[128,4096]{1,0:T(8,128)(2,1)}, f32[128,4096]{1,0:T(8,128)}, f32[1,4096]{1,0:T(1,128)}, f32[1,4096]{1,0:T(1,128)}, f32[16,8,128]{2,1,0:T(8,128)}) custom-call(bf16[128,4096]{1,0:T(8,128)(2,1)} %get-tuple-element.19.emb_ref, bf16[128,4096]{1,0:T(8,128)(2,1)} %copy-done.5, bf16[128,4096]{1,0:T(8,128)(2,1)} %bitcast.32, ...), custom_call_target="tpu_custom_call" | custom-call | flops 128974848 | bytes 13631488 | tf_op jit(solution)/shard_map/pallas_call | solution.py:273
  64.3 0.9 %reduce_sum.39 = f32[16,8]{1,0:T(8,128)S(1)} reduce(f32[16,8,128]{2,1,0:T(8,128)} %get-tuple-element.11, f32[]{:T(128)} %constant.4.clone.1), dimensions={2}, to_apply=%region_3.4 | reduce | flops 16256 | bytes 66052 | tf_op jit(solution)/shard_map/reduce_sum | solution.py:305
  65.3 1.3 %collective-permute-start.4 = (f32[16,8]{1,0:T(8,128)S(1)}, f32[16,8]{1,0:T(8,128)S(1)}, u32[]{:S(2)}, u32[]{:S(2)}) collective-permute-start(f32[16,8]{1,0:T(8,128)S(1)} %reduce_sum.39), channel_id=1, source_target_pairs={{0,1},{1,0},{2,3},{3,2},{4,5},{5,4},{6,7},{7,6},{8,9},{9,8},{10,11... | collective-permute-start | bytes 1544 | tf_op jit(solution)/shard_map/ppermute | solution.py:26
  66.5 1.3 %collective-permute-done.4 = f32[16,8]{1,0:T(8,128)S(1)} collective-permute-done((f32[16,8]{1,0:T(8,128)S(1)}, f32[16,8]{1,0:T(8,128)S(1)}, u32[]{:S(2)}, u32[]{:S(2)}) %collective-permute-start.4) | collective-permute-done | bytes 544 | tf_op jit(solution)/shard_map/ppermute | solution.py:26
  67.8 0.1 copy.13
  67.9 0.1 reshape.42
  68.0 0.0 copy-done.1
  68.0 0.0 copy-start.3
  68.0 3.0 %fusion.3 = bf16[1,128,4096]{2,1,0:T(8,128)(2,1)} fusion(f32[128,4096]{1,0:T(8,128)} %get-tuple-element.10, f32[128]{0:T(128)S(1)} %fusion.8, bf16[1,128,4096]{2,1,0:T(8,128)(2,1)S(1)} %copy-done.1), kind=kLoop, calls=%fused_computation.8 | loop fusion | flops 2097152 | bytes 4194816 | tf_op jit(solution)/shard_map/broadcast_in_dim | solution.py:308
  71.0 0.0 copy-done.3
  71.0 0.0 copy-start.7
  71.0 0.0 copy-start.6
  71.0 1.0 %copy.17 = bf16[1,128,4096]{2,1,0:T(8,128)(2,1)} copy(bf16[1,128,4096]{2,1,0:T(8,128)(2,1)S(1)} %bitcast.33) | data formatting | bytes 2097152
  72.0 0.0 copy-done.7
  72.0 0.6 copy.18
  72.6 0.0 copy-done.6
  72.6 0.6 copy.19
  (7 shorter events, 0.1 us)
Async XLA Ops:
  0.6 9.7 %copy-start.2 = (bf16[1,2,128,4096]{3,2,1,0:T(8,128)(2,1)S(1)}, bf16[1,2,128,4096]{3,2,1,0:T(8,128)(2,1)}, u32[]{:S(2)}) copy-start(bf16[1,2,128,4096]{3,2,1,0:T(8,128)(2,1)} %param.11) | copy-start | bytes 6291460
  0.6 10.0 %copy-start.8 = (s32[128]{0:T(128)S(1)}, s32[128]{0:T(128)}, u32[]{:S(2)}) copy-start(s32[128]{0:T(128)} %param.9) | copy-start | bytes 1540
  3.9 18.5 %collective-permute-start.1 = (bf16[128,4096]{1,0:T(8,128)(2,1)}, bf16[128,4096]{1,0:T(8,128)(2,1)S(1)}, u32[]{:S(2)}, u32[]{:S(2)}) collective-permute-start(bf16[128,4096]{1,0:T(8,128)(2,1)} %get-tuple-element.14), channel_id=1, source_target_pairs={{8,0},{16,8},{24,16},{9,1},{17,9},{25,17},{10,2},{18,10},{26,18},{... | collective-permute-start | bytes 3145736 | tf_op jit(solution)/shard_map/ppermute | solution.py:21
  5.8 16.6 %collective-permute-start = (bf16[128,4096]{1,0:T(8,128)(2,1)}, bf16[128,4096]{1,0:T(8,128)(2,1)S(1)}, u32[]{:S(2)}, u32[]{:S(2)}) collective-permute-start(bf16[128,4096]{1,0:T(8,128)(2,1)} %get-tuple-element.15), channel_id=1, source_target_pairs={{0,8},{8,16},{16,24},{1,9},{9,17},{17,25},{2,10},{10,18},{18,26},{... | collective-permute-start | bytes 3145736 | tf_op jit(solution)/shard_map/ppermute | solution.py:21
  10.6 4.1 %copy-start = (bf16[1,128,4096]{2,1,0:T(8,128)(2,1)S(1)}, bf16[1,128,4096]{2,1,0:T(8,128)(2,1)}, u32[]{:S(2)}) copy-start(bf16[1,128,4096]{2,1,0:T(8,128)(2,1)} %param.12) | copy-start | bytes 3145732
  15.0 2.5 %collective-permute-start.2 = (f32[3,128]{1,0:T(4,128)S(1)}, f32[3,128]{1,0:T(4,128)S(1)}, u32[]{:S(2)}, u32[]{:S(2)}) collective-permute-start(f32[3,128]{1,0:T(4,128)S(1)} %pad_maximum_fusion), channel_id=1, source_target_pairs={{0,1},{1,0},{2,3},{3,2},{4,5},{5,4},{6,7},{7,6},{8,9},{9,8},{10,11... | collective-permute-start | bytes 4616 | tf_op jit(solution)/shard_map/ppermute | solution.py:26
  17.5 4.9 %collective-permute-start.3 = (f32[128]{0:T(128)S(1)}, f32[128]{0:T(128)S(1)}, u32[]{:S(2)}, u32[]{:S(2)}) collective-permute-start(f32[128]{0:T(128)S(1)} %get-tuple-element.16), channel_id=1, source_target_pairs={{0,8},{8,16},{16,24},{1,9},{9,17},{17,25},{2,10},{10,18},{18,26},{... | collective-permute-start | bytes 1544 | tf_op jit(solution)/shard_map/ppermute | solution.py:21
  22.4 1.0 %copy-start.4 = (bf16[128,4096]{1,0:T(8,128)(2,1)}, bf16[128,4096]{1,0:T(8,128)(2,1)S(1)}, u32[]{:S(2)}) copy-start(bf16[128,4096]{1,0:T(8,128)(2,1)S(1)} %collective-permute-done.1.ret_ref) | copy-start | bytes 3145732
  22.4 1.3 %copy-start.5 = (bf16[128,4096]{1,0:T(8,128)(2,1)}, bf16[128,4096]{1,0:T(8,128)(2,1)S(1)}, u32[]{:S(2)}) copy-start(bf16[128,4096]{1,0:T(8,128)(2,1)S(1)} %collective-permute-done.arr_ref) | copy-start | bytes 3145732
  23.8 44.2 %copy-start.1 = (bf16[1,128,4096]{2,1,0:T(8,128)(2,1)S(1)}, bf16[1,128,4096]{2,1,0:T(8,128)(2,1)}, u32[]{:S(2)}) copy-start(bf16[1,128,4096]{2,1,0:T(8,128)(2,1)} %param.12) | copy-start | bytes 3145732
  65.3 2.6 %collective-permute-start.4 = (f32[16,8]{1,0:T(8,128)S(1)}, f32[16,8]{1,0:T(8,128)S(1)}, u32[]{:S(2)}, u32[]{:S(2)}) collective-permute-start(f32[16,8]{1,0:T(8,128)S(1)} %reduce_sum.39), channel_id=1, source_target_pairs={{0,1},{1,0},{2,3},{3,2},{4,5},{5,4},{6,7},{7,6},{8,9},{9,8},{10,11... | collective-permute-start | bytes 1544 | tf_op jit(solution)/shard_map/ppermute | solution.py:26
  68.0 3.0 %copy-start.3 = (bf16[128,4096]{1,0:T(8,128)(2,1)S(1)}, bf16[128,4096]{1,0:T(8,128)(2,1)}, u32[]{:S(2)}) copy-start(bf16[128,4096]{1,0:T(8,128)(2,1)} %get-tuple-element.9) | copy-start | bytes 3145732
  71.0 1.0 %copy-start.7 = (f32[1,4096]{1,0:T(1,128)S(1)}, f32[1,4096]{1,0:T(1,128)}, u32[]{:S(2)}) copy-start(f32[1,4096]{1,0:T(1,128)} %get-tuple-element.12) | copy-start | bytes 49156
  71.0 1.6 %copy-start.6 = (f32[1,4096]{1,0:T(1,128)S(1)}, f32[1,4096]{1,0:T(1,128)}, u32[]{:S(2)}) copy-start(f32[1,4096]{1,0:T(1,128)} %get-tuple-element.13) | copy-start | bytes 49156

commit v4 on v3

--- a/solution.py
+++ b/solution.py
@@ -15,12 +15,6 @@
 epsilon = 1e-06
 
 
-def shifted(value, axis, steps):
-    count = lax.axis_size(axis)
-    initial, last = (max(0, -steps), min(count, count - steps))
-    return lax.ppermute(value, axis, [(source, source + steps) for source in range(initial, last)])
-
-
 def width_sum(value):
     if lax.axis_size("width") == 2:
         return value + lax.ppermute(value, "width", [(0, 1), (1, 0)])
@@ -31,10 +25,21 @@
     return jnp.broadcast_to(row, (ROWS, LANES))
 
 
-def step_kernel(segments, emb_ref, arr_ref, sav_ref, loss_ref, ret_ref, scale_ref, gain_ref,
+def summed(terms):
+    sums = terms[:4]
+    for index, term in enumerate(terms[4:]):
+        sums[index % 4] = sums[index % 4] + term
+    total = sums[0]
+    for term in sums[1:]:
+        total = total + term
+    return total
+
+
+def step_kernel(segments, bound_ref, emb_ref, sav_ref, loss_ref, square_ref, gain_ref,
                 decay_ref, skip_ref, residue_ref,
                 out_ref, part_ref, gg_ref, sg_ref, acc_ref,
-                sig, res, last, e_all, end_ref, recv_ref, send_sem, recv_sem):
+                sig, res, last, e_all, end_ref, recv_ref, rows_ref, scale_ref, came_ref,
+                send_sem, recv_sem, row_send, row_recv, tile_sem):
     peers = recv_ref.shape[0] + 1
     mine = lax.axis_index("ctx")
     segment = lax.axis_index("pipe")
@@ -46,13 +51,36 @@
     steps = length // ROWS
     modes = decay_ref.shape[0]
 
-    def incoming(lanes):
-        return jnp.where(segment == 0, emb_ref[:, lanes].astype(jnp.float32),
-                         arr_ref[:, lanes].astype(jnp.float32))
-
-    def cotangent(lanes):
-        return jnp.where(segment == segments - 1, loss_ref[:, lanes].astype(jnp.float32),
-                         ret_ref[:, lanes].astype(jnp.float32))
+    def incoming(here):
+        return rows_ref[1, :, here].astype(jnp.float32)
+
+    def cotangent(here):
+        return rows_ref[0, :, here].astype(jnp.float32)
+
+    def move(c, forward):
+        lanes = pl.ds(pl.multiple_of(c * chunk, chunk), chunk)
+        target = jnp.minimum(segment + 1, segments - 1) if forward else jnp.maximum(segment - 1, 0)
+        return pltpu.make_async_remote_copy(
+            src_ref=bound_ref.at[0, forward, :, lanes],
+            dst_ref=rows_ref.at[forward, :, lanes],
+            send_sem=row_send.at[c, forward],
+            recv_sem=row_recv.at[c, forward],
+            device_id={"pipe": target},
+            device_id_type=pl.DeviceIdType.MESH,
+        )
+
+    def move_tile():
+        return pltpu.make_async_remote_copy(
+            src_ref=square_ref.at[0],
+            dst_ref=came_ref,
+            send_sem=tile_sem.at[0],
+            recv_sem=tile_sem.at[1],
+            device_id={"pipe": jnp.minimum(segment + 1, segments - 1)},
+            device_id_type=pl.DeviceIdType.MESH,
+        )
+
+    first = segment == 0
+    final = segment == segments - 1
 
     def copy(c, far, rev):
         lanes = pl.ds(pl.multiple_of(c * chunk, chunk), chunk)
@@ -73,22 +101,81 @@
         for far in range(1, peers):
             pl.semaphore_signal(barrier, inc=1, device_id={"ctx": lax.rem(mine + far, peers)},
                                 device_id_type=pl.DeviceIdType.MESH)
-        pl.semaphore_wait(barrier, peers - 1)
+
+        @pl.when(jnp.logical_not(first))
+        def _():
+            pl.semaphore_signal(barrier, inc=1, device_id={"pipe": jnp.maximum(segment - 1, 0)},
+                                device_id_type=pl.DeviceIdType.MESH)
+
+        @pl.when(jnp.logical_not(final))
+        def _():
+            pl.semaphore_signal(barrier, inc=1,
+                                device_id={"pipe": jnp.minimum(segment + 1, segments - 1)},
+                                device_id_type=pl.DeviceIdType.MESH)
+
+        around = jnp.where(first, 0, 1) + jnp.where(final, 0, 1)
+        pl.semaphore_wait(barrier, peers - 1 + around)
+
+        @pl.when(jnp.logical_not(final))
+        def _():
+            move_tile().start()
+
+        for c in range(chunks):
+            @pl.when(jnp.logical_not(final))
+            def _():
+                move(c, 1).start()
+
+            @pl.when(jnp.logical_not(first))
+            def _():
+                move(c, 0).start()
+
         acc_ref[...] = jnp.zeros_like(acc_ref)
+        scale_ref[1] = lax.rsqrt(square_ref[1] / D + epsilon)
+
+        @pl.when(first)
+        def _():
+            scale_ref[0] = lax.rsqrt(square_ref[2] / D + epsilon)
+
+        @pl.when(jnp.logical_not(first))
+        def _():
+            move_tile().wait_recv()
+            scale_ref[0] = lax.rsqrt(came_ref[...] / D + epsilon)
+
+        @pl.when(jnp.logical_not(final))
+        def _():
+            move_tile().wait_send()
 
     @pl.when(step < chunks)
     def _():
+        block = pl.ds(pl.multiple_of(step * chunk, chunk), chunk)
+
+        @pl.when(first)
+        def _():
+            rows_ref[1, :, block] = emb_ref[...]
+
+        @pl.when(jnp.logical_not(first))
+        def _():
+            move(step, 1).wait_recv()
+
+        @pl.when(final)
+        def _():
+            rows_ref[0, :, block] = loss_ref[...]
+
+        @pl.when(jnp.logical_not(final))
+        def _():
+            move(step, 0).wait_recv()
+
         place = lax.broadcasted_iota(jnp.int32, (ROWS, LANES), 0)
 
         def group(g, carry):
             lanes = pl.ds(pl.multiple_of(g * LANES, LANES), LANES)
+            here = pl.ds(pl.multiple_of(step * chunk + g * LANES, LANES), LANES)
             gain = gain_ref[:, lanes]
             back = sav_ref[:, lanes].astype(jnp.float32) * sb_ref[...] * gain
-            sig[0] = incoming(lanes) * sf_ref[...] * gain
+            sig[0] = incoming(here) * sf_ref[...] * gain
             sig[1] = back
-            sig[2] = cotangent(lanes) * back
+            sig[2] = cotangent(here) * back
             damping = decay_ref[:, lanes]
-            here = pl.ds(pl.multiple_of(step * chunk + g * LANES, LANES), LANES)
             a_all = jnp.exp(-damping)
             stride_all = jnp.exp(-damping * float(steps))
             a = [wide(a_all[k:k + 1]) for k in range(modes)]
@@ -136,6 +223,15 @@
         place = lax.broadcasted_iota(jnp.int32, (ROWS, LANES), 0).astype(jnp.float32)
 
         c = step - chunks
+
+        @pl.when(jnp.logical_not(final))
+        def _():
+            move(c, 1).wait_send()
+
+        @pl.when(jnp.logical_not(first))
+        def _():
+            move(c, 0).wait_send()
+
         for far in range(1, peers):
             @pl.when(mine + far < peers)
             def _():
@@ -149,15 +245,15 @@
 
         def group(g, carry):
             lanes = pl.ds(pl.multiple_of(g * LANES, LANES), LANES)
+            here = pl.ds(pl.multiple_of(c * chunk + g * LANES, LANES), LANES)
             gain = gain_ref[:, lanes]
             gain_w = wide(gain)
-            sig[0] = incoming(lanes)
+            sig[0] = incoming(here)
             sig[1] = sav_ref[:, lanes].astype(jnp.float32) * sb_ref[...]
-            sig[2] = cotangent(lanes)
+            sig[2] = cotangent(here)
             damping = decay_ref[:, lanes]
             a_all = jnp.exp(-damping)
             coefs = residue_ref[:, lanes] * jnp.sqrt(1.0 - jnp.exp(-2.0 * damping))
-            here = pl.ds(pl.multiple_of(c * chunk + g * LANES, LANES), LANES)
             whole = jnp.exp(-damping * float(length))
             entering = []
             for q in range(3):
@@ -179,6 +275,10 @@
 
             def conv(q, pieces, emit):
                 rev = q == 2
+                near = []
+                for n in range(steps):
+                    near.append(summed([kernel[n - m] * pieces[steps - 1 - m if rev else m]
+                                        for m in range(n + 1)]))
                 ago = (float(ROWS - 1) - place) if rev else place
                 decayed = []
                 for k in range(modes):
@@ -188,12 +288,7 @@
                 a = [wide(a_all[k:k + 1]) for k in range(modes)]
                 for n in range(steps):
                     decayed = [a[k] * decayed[k] for k in range(modes)]
-                    terms = decayed + [kernel[n - m] * pieces[steps - 1 - m if rev else m]
-                                       for m in range(n + 1)]
-                    sums = terms[:4]
-                    for index, term in enumerate(terms[4:]):
-                        sums[index % 4] = sums[index % 4] + term
-                    emit(steps - 1 - n if rev else n, (sums[0] + sums[1]) + (sums[2] + sums[3]))
+                    emit(steps - 1 - n if rev else n, summed([near[n]] + decayed))
 
             raw = [sig[0, rows(i), :] for i in range(steps)]
             normed = [raw[i] * sf_ref[rows(i), :] * gain_w for i in range(steps)]
@@ -235,10 +330,7 @@
 
 
 def local(tokens, table, boundary, saved_in, loss_grad, gain, skip, residue, decay_rate):
-    segment_index = lax.axis_index("pipe")
     segments = lax.axis_size("pipe")
-    arrived = shifted(boundary[0, 1], "pipe", 1)
-    returned = shifted(boundary[0, 0], "pipe", -1)
     onehot = (tokens[:, None] == jnp.arange(table.shape[0], dtype=jnp.int32)[None, :]).astype(
         jnp.bfloat16
     )
@@ -252,12 +344,11 @@
     squares = width_sum(
         jnp.stack([squares_of(boundary[0, 1]), squares_of(sav), squares_of(embedded)])
     )
-    square_fwd = jnp.where(segment_index == 0, squares[2], shifted(squares[0], "pipe", 1))
-    scales = lax.rsqrt(jnp.stack([square_fwd, squares[1]]) / D + epsilon)
     length, channels = sav.shape
     modes = decay_rate.shape[1]
     steps = length // ROWS
-    scale_tiles = jnp.broadcast_to(scales[:, :, None], (2, length, LANES))
+    squares_wide = jnp.broadcast_to(squares[:, :, None], (3, length, LANES))
+    scale_back = lax.rsqrt(squares[1] / D + epsilon)
     chunk = min(CHUNK, channels)
     chunks = channels // chunk
     peers = lax.axis_size("ctx")
@@ -267,6 +358,9 @@
     def both(height):
         return pl.BlockSpec((height, chunk), lambda s: (0, lax.rem(s, chunks)))
 
+    def early(height):
+        return pl.BlockSpec((height, chunk), lambda s: (0, jnp.minimum(s, chunks - 1)))
+
     def late(height):
         return pl.BlockSpec((height, chunk), lambda s: (0, jnp.maximum(s - chunks, 0)))
 
@@ -274,8 +368,8 @@
         functools.partial(step_kernel, segments),
         grid=(2 * chunks,),
         in_specs=[
-            both(length), both(length), both(length), both(length), both(length),
-            pl.BlockSpec((2, length, LANES), lambda s: (0, 0, 0)),
+            pl.BlockSpec(memory_space=pl.ANY), early(length), both(length), early(length),
+            pl.BlockSpec((3, length, LANES), lambda s: (0, 0, 0)),
             both(1), both(modes), late(1), late(modes),
         ],
         out_specs=[late(length), late(length), late(1), late(1),
@@ -294,16 +388,22 @@
             pltpu.VMEM((3, modes, ROWS, channels), f32),
             pltpu.VMEM((3, modes, channels), jnp.bfloat16),
             pltpu.VMEM((peers - 1, 3, modes, channels), jnp.bfloat16),
+            pltpu.VMEM((2, length, channels), jnp.bfloat16),
+            pltpu.VMEM((2, length, LANES), f32),
+            pltpu.VMEM((length, LANES), f32),
             pltpu.SemaphoreType.DMA((chunks, 2 * (peers - 1))),
             pltpu.SemaphoreType.DMA((chunks, 2 * (peers - 1))),
+            pltpu.SemaphoreType.DMA((chunks, 2)),
+            pltpu.SemaphoreType.DMA((chunks, 2)),
+            pltpu.SemaphoreType.DMA((2,)),
         ],
         compiler_params=pltpu.CompilerParams(
             vmem_limit_bytes=VMEM, collective_id=0, has_side_effects=True
         ),
         cost_estimate=pl.CostEstimate(flops=246 * work, bytes_accessed=26 * work, transcendentals=0),
-    )(embedded, arrived, sav, loss_grad, returned, scale_tiles, gain, decay_rate[0], skip, residue[0])
+    )(boundary, embedded, sav, loss_grad, squares_wide, gain, decay_rate[0], skip, residue[0])
     inner_sum = width_sum(jnp.sum(inner, axis=2)).T.reshape(length)
-    factor = (scales[1] ** 2 * inner_sum / D)[:, None]
+    factor = (scale_back ** 2 * inner_sum / D)[:, None]
     input_grad = (part - sav.astype(f32) * factor).astype(jnp.bfloat16)
     return (out[None], input_grad[None], gain_grad[None], skip_grad[None])
 

time: 74.7 us -> 66.8 us (0.89); the launches traced: 73.2 us -> 66.5 us
  starting transfers between devices: 12.6 us -> 3.38 us
  Pallas kernels: 40.6 us -> 46.1 us
  local copies, waits for them, and re-layouts: 6.92 us -> 3.15 us
  other arithmetic: 4.52 us -> 6.98 us
  waiting for transfers between devices: 3.74 us -> 2.26 us
    ppermute x3 -> x0, starting transfers between devices: 10.1 us -> none  [shifted(): lax.ppermute(value, axis, [(source, source + steps) for source in range(i...]
    pallas_call x1, Pallas kernels: 40.6 us -> 46.1 us  [local(): pl.pallas_call(functools.partial(step_kernel, segments), grid=(2 * chunks...]
    squeeze x2 -> x0, local copies, waits for them, and re-layouts: 3.23 us -> none  [the longest x1 3.22 us: local(): returned = shifted(boundary[0, 0], 'pipe', -1)]
    reduce_sum x2, other arithmetic: 0.57 us -> 3.04 us  [squares_of(): return jnp.sum(value * value, axis=1)]
    ppermute x3 -> x0, waiting for transfers between devices: 1.23 us -> none  [shifted(): lax.ppermute(value, axis, [(source, source + steps) for source in range(i...]
    ppermute x2, starting transfers between devices: 2.55 us -> 3.38 us  [width_sum(): return value + lax.ppermute(value, 'width', [(0, 1), (1, 0)])]
    unnamed x21 -> x13, local copies, waits for them, and re-layouts: 2.65 us -> 2.2 us
  transfers between devices with their start and end apart: 5 -> 2, of which waited for: 3 -> 2; matrix products, arithmetic and copies ran while one was open for 6% -> 0% of each run, Pallas kernels for 0% -> 0%
where the time goes in v4:
time: 66.8 us; the launch traced here: 66.5 us
  Pallas kernels  46.1 us (69%)
  other arithmetic  6.98 us (10%)
  matrix products  3.96 us (6%)
  starting transfers between devices  3.38 us (5%)
  local copies, waits for them, and re-layouts  3.15 us (5%)
  waiting for transfers between devices  2.26 us (3%)
  between operations  0.68 us (1%)
    pallas_call x1, Pallas kernels, local(): pl.pallas_call(functools.partial(step_kernel, segments), grid=(2 * chunks...  46.1 us
    dot_general x1, matrix products, local(): jnp.dot(onehot, table, preferred_element_type=jnp.float32)  3.96 us
    ppermute x2, starting transfers between devices, width_sum(): return value + lax.ppermute(value, 'width', [(0, 1), (1, 0)])  3.38 us
    reduce_sum x2, other arithmetic, squares_of(): return jnp.sum(value * value, axis=1)  3.04 us
    broadcast_in_dim x1, other arithmetic, local(): return (out[None], input_grad[None], gain_grad[None], skip_grad[None])  2.98 us
    ppermute x2, waiting for transfers between devices, width_sum(): return value + lax.ppermute(value, 'width', [(0, 1), (1, 0)])  2.26 us
    unnamed x13, local copies, waits for them, and re-layouts  2.2 us
  transfers between devices with their start and end apart: 2, of which 2 were waited for; matrix products, arithmetic and copies ran while one was open for 0% of the time, Pallas kernels for 0%

profile of v4, /device:TPU:1, one launch (start us, length us, event | category | flops | bytes accessed | tf_op | source)
XLA Modules:
  0.0 66.5 jit_solution(14652245420685028890)
XLA Ops:
  0.6 0.0 copy-start.4
  0.6 1.5 %multiply_reduce_fusion.1 = f32[128]{0:T(128)S(1)} fusion(bf16[1,2,128,4096]{3,2,1,0:T(8,128)(2,1)} %bound_ref.1), kind=kLoop, calls=%fused_computation.7 | loop fusion | flops 1572736 | bytes 1049088 | tf_op jit(solution)/shard_map/reduce_sum | solution.py:342
  2.2 1.5 %fusion = f32[128]{0:T(128)S(1)} fusion(bf16[1,128,4096]{2,1,0:T(8,128)(2,1)} %param.12), kind=kLoop, calls=%fused_computation.3 | loop fusion | flops 1572736 | bytes 1049088 | tf_op jit(solution)/shard_map/reduce_sum | solution.py:342
  3.7 0.0 copy-done.4
  3.7 4.0 %multiply_reduce_fusion = (f32[128]{0:T(128)S(1)}, bf16[128,4096]{1,0:T(8,128)(2,1)}) fusion(bf16[512,4096]{1,0:T(8,128)(2,1)} %param.10, s32[128]{0:T(128)S(1)} %copy-done.4), kind=kOutput, calls=%fused_computation.6 | convolution fusion | flops 539033472 | bytes 5243904 | tf_op jit(solution)/shard_map/dot_general | solution.py:337
  7.7 2.1 %collective-permute-start = (f32[3,128]{1,0:T(4,128)S(1)}, f32[3,128]{1,0:T(4,128)S(1)}, u32[]{:S(2)}, u32[]{:S(2)}) collective-permute-start(f32[3,128]{1,0:T(4,128)S(1)} %pad_maximum_fusion), channel_id=1, source_target_pairs={{0,1},{1,0},{2,3},{3,2},{4,5},{5,4},{6,7},{7,6},{8,9},{9,8},{10,11... | collective-permute-start | bytes 4616 | tf_op jit(solution)/shard_map/ppermute | solution.py:20
  9.8 1.0 %collective-permute-done = f32[3,128]{1,0:T(4,128)S(1)} collective-permute-done((f32[3,128]{1,0:T(4,128)S(1)}, f32[3,128]{1,0:T(4,128)S(1)}, u32[]{:S(2)}, u32[]{:S(2)}) %collective-permute-start) | collective-permute-done | bytes 1568 | tf_op jit(solution)/shard_map/ppermute | solution.py:20
  10.7 0.8 %broadcast_in_dim.10.square_ref = f32[3,128,128]{2,1,0:T(8,128)} broadcast(f32[3,128]{1,0:T(4,128)S(1)} %fusion.6), dimensions={0,1} | broadcast | bytes 198144 | tf_op jit(solution)/shard_map/broadcast_in_dim | solution.py:350
  11.5 0.0 copy-start
  11.5 46.1 %shard_map.120 = (bf16[128,4096]{1,0:T(8,128)(2,1)}, f32[128,4096]{1,0:T(8,128)}, f32[1,4096]{1,0:T(1,128)}, f32[1,4096]{1,0:T(1,128)}, f32[16,8,128]{2,1,0:T(8,128)}) custom-call(bf16[1,2,128,4096]{3,2,1,0:T(8,128)(2,1)} %bound_ref.1, bf16[128,4096]{1,0:T(8,128)(2,1)} %get-tuple-element.15.emb_ref, bf16[128,4096]{1,0:T(8,128)(2,1)} %bitcast.20, ...), custom_call_target="tpu_custom_call" | custom-call | flops 128974848 | bytes 13631488 | tf_op jit(solution)/shard_map/pallas_call | solution.py:367
  57.7 0.9 %reduce_sum.39 = f32[16,8]{1,0:T(8,128)S(1)} reduce(f32[16,8,128]{2,1,0:T(8,128)} %get-tuple-element.11, f32[]{:T(128)} %constant.2.clone.1), dimensions={2}, to_apply=%region_3.0 | reduce | flops 16256 | bytes 66052 | tf_op jit(solution)/shard_map/reduce_sum | solution.py:405
  58.6 1.3 %collective-permute-start.1 = (f32[16,8]{1,0:T(8,128)S(1)}, f32[16,8]{1,0:T(8,128)S(1)}, u32[]{:S(2)}, u32[]{:S(2)}) collective-permute-start(f32[16,8]{1,0:T(8,128)S(1)} %reduce_sum.39), channel_id=1, source_target_pairs={{0,1},{1,0},{2,3},{3,2},{4,5},{5,4},{6,7},{7,6},{8,9},{9,8},{10,11... | collective-permute-start | bytes 1544 | tf_op jit(solution)/shard_map/ppermute | solution.py:20
  59.9 1.3 %collective-permute-done.1 = f32[16,8]{1,0:T(8,128)S(1)} collective-permute-done((f32[16,8]{1,0:T(8,128)S(1)}, f32[16,8]{1,0:T(8,128)S(1)}, u32[]{:S(2)}, u32[]{:S(2)}) %collective-permute-start.1) | collective-permute-done | bytes 544 | tf_op jit(solution)/shard_map/ppermute | solution.py:20
  61.2 0.1 copy.13
  61.2 0.1 reshape.35
  61.3 0.0 copy-done
  61.3 0.0 copy-start.1
  61.3 3.0 %fusion.3 = bf16[1,128,4096]{2,1,0:T(8,128)(2,1)} fusion(f32[128,4096]{1,0:T(8,128)} %get-tuple-element.10, f32[128]{0:T(128)S(1)} %fusion.5, bf16[1,128,4096]{2,1,0:T(8,128)(2,1)S(1)} %copy-done), kind=kLoop, calls=%fused_computation.8 | loop fusion | flops 2097152 | bytes 4194816 | tf_op jit(solution)/shard_map/broadcast_in_dim | solution.py:408
  64.3 0.0 copy-done.1
  64.3 0.0 copy-start.3
  64.3 0.0 copy-start.2
  64.3 1.0 %copy.17 = bf16[1,128,4096]{2,1,0:T(8,128)(2,1)} copy(bf16[1,128,4096]{2,1,0:T(8,128)(2,1)S(1)} %bitcast.21) | data formatting | bytes 2097152
  65.3 0.0 copy-done.3
  65.3 0.6 copy.18
  65.9 0.0 copy-done.2
  65.9 0.6 copy.19
  (4 shorter events, 0.0 us)
Async XLA Ops:
  0.6 3.1 %copy-start.4 = (s32[128]{0:T(128)S(1)}, s32[128]{0:T(128)}, u32[]{:S(2)}) copy-start(s32[128]{0:T(128)} %param.9) | copy-start | bytes 1540
  7.7 3.1 %collective-permute-start = (f32[3,128]{1,0:T(4,128)S(1)}, f32[3,128]{1,0:T(4,128)S(1)}, u32[]{:S(2)}, u32[]{:S(2)}) collective-permute-start(f32[3,128]{1,0:T(4,128)S(1)} %pad_maximum_fusion), channel_id=1, source_target_pairs={{0,1},{1,0},{2,3},{3,2},{4,5},{5,4},{6,7},{7,6},{8,9},{9,8},{10,11... | collective-permute-start | bytes 4616 | tf_op jit(solution)/shard_map/ppermute | solution.py:20
  11.5 49.8 %copy-start = (bf16[1,128,4096]{2,1,0:T(8,128)(2,1)S(1)}, bf16[1,128,4096]{2,1,0:T(8,128)(2,1)}, u32[]{:S(2)}) copy-start(bf16[1,128,4096]{2,1,0:T(8,128)(2,1)} %param.12) | copy-start | bytes 3145732
  58.6 2.6 %collective-permute-start.1 = (f32[16,8]{1,0:T(8,128)S(1)}, f32[16,8]{1,0:T(8,128)S(1)}, u32[]{:S(2)}, u32[]{:S(2)}) collective-permute-start(f32[16,8]{1,0:T(8,128)S(1)} %reduce_sum.39), channel_id=1, source_target_pairs={{0,1},{1,0},{2,3},{3,2},{4,5},{5,4},{6,7},{7,6},{8,9},{9,8},{10,11... | collective-permute-start | bytes 1544 | tf_op jit(solution)/shard_map/ppermute | solution.py:20
  61.3 3.0 %copy-start.1 = (bf16[128,4096]{1,0:T(8,128)(2,1)S(1)}, bf16[128,4096]{1,0:T(8,128)(2,1)}, u32[]{:S(2)}) copy-start(bf16[128,4096]{1,0:T(8,128)(2,1)} %get-tuple-element.9) | copy-start | bytes 3145732
  64.3 1.0 %copy-start.3 = (f32[1,4096]{1,0:T(1,128)S(1)}, f32[1,4096]{1,0:T(1,128)}, u32[]{:S(2)}) copy-start(f32[1,4096]{1,0:T(1,128)} %get-tuple-element.12) | copy-start | bytes 49156
  64.3 1.6 %copy-start.2 = (f32[1,4096]{1,0:T(1,128)S(1)}, f32[1,4096]{1,0:T(1,128)}, u32[]{:S(2)}) copy-start(f32[1,4096]{1,0:T(1,128)} %get-tuple-element.13) | copy-start | bytes 49156

commit v5 on v4

--- a/solution.py
+++ b/solution.py
@@ -310,7 +310,7 @@
             skip_sum = mix[0] * back[0]
             for i in range(1, steps):
                 skip_sum = skip_sum + mix[i] * back[i]
-            sg_ref[:, lanes] = jnp.sum(skip_sum, axis=0, keepdims=True)
+            sg_ref[:, lanes] = skip_sum
             gain_sums = [jnp.zeros((ROWS, LANES), jnp.float32)]
 
             def emit_grad(i, value):
@@ -323,7 +323,7 @@
 
             conv(2, mix, emit_grad)
             part_ref[:, lanes] = res[2]
-            gg_ref[:, lanes] = jnp.sum(gain_sums[0], axis=0, keepdims=True)
+            gg_ref[:, lanes] = gain_sums[0]
             return carry
 
         lax.fori_loop(0, chunk // LANES, group, 0)
@@ -372,13 +372,13 @@
             pl.BlockSpec((3, length, LANES), lambda s: (0, 0, 0)),
             both(1), both(modes), late(1), late(modes),
         ],
-        out_specs=[late(length), late(length), late(1), late(1),
+        out_specs=[late(length), late(length), late(ROWS), late(ROWS),
                    pl.BlockSpec((steps, ROWS, LANES), lambda s: (0, 0, 0))],
         out_shape=[
             jax.ShapeDtypeStruct((length, channels), jnp.bfloat16),
             jax.ShapeDtypeStruct((length, channels), f32),
-            jax.ShapeDtypeStruct((1, channels), f32),
-            jax.ShapeDtypeStruct((1, channels), f32),
+            jax.ShapeDtypeStruct((ROWS, channels), f32),
+            jax.ShapeDtypeStruct((ROWS, channels), f32),
             jax.ShapeDtypeStruct((steps, ROWS, LANES), f32),
         ],
         scratch_shapes=[
@@ -402,10 +402,11 @@
         ),
         cost_estimate=pl.CostEstimate(flops=246 * work, bytes_accessed=26 * work, transcendentals=0),
     )(boundary, embedded, sav, loss_grad, squares_wide, gain, decay_rate[0], skip, residue[0])
+    grads = [jnp.sum(rows, axis=0)[None, None, :] for rows in (gain_grad, skip_grad)]
     inner_sum = width_sum(jnp.sum(inner, axis=2)).T.reshape(length)
     factor = (scale_back ** 2 * inner_sum / D)[:, None]
     input_grad = (part - sav.astype(f32) * factor).astype(jnp.bfloat16)
-    return (out[None], input_grad[None], gain_grad[None], skip_grad[None])
+    return (out[None], input_grad[None], grads[0], grads[1])
 
 
 def solution(mesh):

time: 66.8 us -> 67.3 us (level)
  other arithmetic: 6.98 us -> 10.1 us
  waiting for transfers between devices: 2.26 us -> 0.98 us
  local copies, waits for them, and re-layouts: 3.15 us -> 1.93 us
    reduce_sum x0 -> x2, other arithmetic: none -> 3.08 us  [local(): jnp.sum(rows, axis=0)[None, None, :]]
    ppermute x2, waiting for transfers between devices: 2.26 us -> 0.98 us  [width_sum(): return value + lax.ppermute(value, 'width', [(0, 1), (1, 0)])]
    unnamed x13 -> x7, local copies, waits for them, and re-layouts: 2.2 us -> 0.98 us
  transfers between devices with their start and end apart: 2 -> 2, of which waited for: 2 -> 1; matrix products, arithmetic and copies ran while one was open for 0% -> 5% of each run, Pallas kernels for 0% -> 0%
where the time goes in v5:
time: 67.3 us; the launch traced here: 67 us
  Pallas kernels  46 us (68%)
  other arithmetic  10.1 us (15%)
  matrix products  3.96 us (6%)
  starting transfers between devices  3.38 us (5%)
  local copies, waits for them, and re-layouts  1.93 us (3%)
  waiting for transfers between devices  0.98 us (1%)
  between operations  0.68 us (1%)
    pallas_call x1, Pallas kernels, local(): pl.pallas_call(functools.partial(step_kernel, segments), grid=(2 * chunks...  46 us
    dot_general x1, matrix products, local(): jnp.dot(onehot, table, preferred_element_type=jnp.float32)  3.96 us
    ppermute x2, starting transfers between devices, width_sum(): return value + lax.ppermute(value, 'width', [(0, 1), (1, 0)])  3.38 us
    reduce_sum x2, other arithmetic, local(): jnp.sum(rows, axis=0)[None, None, :]  3.08 us
    reduce_sum x2, other arithmetic, squares_of(): return jnp.sum(value * value, axis=1)  3.04 us
    broadcast_in_dim x1, other arithmetic, local(): return (out[None], input_grad[None], grads[0], grads[1])  2.98 us
  transfers between devices with their start and end apart: 2, of which 1 were waited for; matrix products, arithmetic and copies ran while one was open for 5% of the time, Pallas kernels for 0%

profile of v5, /device:TPU:1, one launch (start us, length us, event | category | flops | bytes accessed | tf_op | source)
XLA Modules:
  0.0 67.0 jit_solution(3579640661228710527)
XLA Ops:
  0.6 0.0 copy-start.2
  0.6 1.5 %multiply_reduce_fusion.1 = f32[128]{0:T(128)S(1)} fusion(bf16[1,2,128,4096]{3,2,1,0:T(8,128)(2,1)} %bound_ref.1), kind=kLoop, calls=%fused_computation.7 | loop fusion | flops 1572736 | bytes 1049088 | tf_op jit(solution)/shard_map/reduce_sum | solution.py:342
  2.2 1.5 %fusion = f32[128]{0:T(128)S(1)} fusion(bf16[1,128,4096]{2,1,0:T(8,128)(2,1)} %param.12), kind=kLoop, calls=%fused_computation.3 | loop fusion | flops 1572736 | bytes 1049088 | tf_op jit(solution)/shard_map/reduce_sum | solution.py:342
  3.7 0.0 copy-done.2
  3.7 4.0 %multiply_reduce_fusion = (f32[128]{0:T(128)S(1)}, bf16[128,4096]{1,0:T(8,128)(2,1)}) fusion(bf16[512,4096]{1,0:T(8,128)(2,1)} %param.10, s32[128]{0:T(128)S(1)} %copy-done.2), kind=kOutput, calls=%fused_computation.6 | convolution fusion | flops 539033472 | bytes 5243904 | tf_op jit(solution)/shard_map/dot_general | solution.py:337
  7.7 2.1 %collective-permute-start = (f32[3,128]{1,0:T(4,128)S(1)}, f32[3,128]{1,0:T(4,128)S(1)}, u32[]{:S(2)}, u32[]{:S(2)}) collective-permute-start(f32[3,128]{1,0:T(4,128)S(1)} %pad_maximum_fusion), channel_id=1, source_target_pairs={{0,1},{1,0},{2,3},{3,2},{4,5},{5,4},{6,7},{7,6},{8,9},{9,8},{10,11... | collective-permute-start | bytes 4616 | tf_op jit(solution)/shard_map/ppermute | solution.py:20
  9.8 1.0 %collective-permute-done = f32[3,128]{1,0:T(4,128)S(1)} collective-permute-done((f32[3,128]{1,0:T(4,128)S(1)}, f32[3,128]{1,0:T(4,128)S(1)}, u32[]{:S(2)}, u32[]{:S(2)}) %collective-permute-start) | collective-permute-done | bytes 1568 | tf_op jit(solution)/shard_map/ppermute | solution.py:20
  10.7 0.8 %broadcast_in_dim.10.square_ref = f32[3,128,128]{2,1,0:T(8,128)} broadcast(f32[3,128]{1,0:T(4,128)S(1)} %fusion.6), dimensions={0,1} | broadcast | bytes 198144 | tf_op jit(solution)/shard_map/broadcast_in_dim | solution.py:350
  11.5 0.0 copy-start
  11.5 46.0 %shard_map.120 = (bf16[128,4096]{1,0:T(8,128)(2,1)}, f32[128,4096]{1,0:T(8,128)}, f32[8,4096]{1,0:T(8,128)}, f32[8,4096]{1,0:T(8,128)}, f32[16,8,128]{2,1,0:T(8,128)}) custom-call(bf16[1,2,128,4096]{3,2,1,0:T(8,128)(2,1)} %bound_ref.1, bf16[128,4096]{1,0:T(8,128)(2,1)} %get-tuple-element.15.emb_ref, bf16[128,4096]{1,0:T(8,128)(2,1)} %bitcast.20, ...), custom_call_target="tpu_custom_call" | custom-call | flops 128974848 | bytes 13631488 | tf_op jit(solution)/shard_map/pallas_call | solution.py:367
  57.6 0.9 %reduce_sum.57 = f32[16,8]{1,0:T(8,128)S(1)} reduce(f32[16,8,128]{2,1,0:T(8,128)} %get-tuple-element.11, f32[]{:T(128)} %constant.2.clone.1), dimensions={2}, to_apply=%region_3.0 | reduce | flops 16256 | bytes 66052 | tf_op jit(solution)/shard_map/reduce_sum | solution.py:406
  58.5 1.3 %collective-permute-start.1 = (f32[16,8]{1,0:T(8,128)S(1)}, f32[16,8]{1,0:T(8,128)S(1)}, u32[]{:S(2)}, u32[]{:S(2)}) collective-permute-start(f32[16,8]{1,0:T(8,128)S(1)} %reduce_sum.57), channel_id=1, source_target_pairs={{0,1},{1,0},{2,3},{3,2},{4,5},{5,4},{6,7},{7,6},{8,9},{9,8},{10,11... | collective-permute-start | bytes 1544 | tf_op jit(solution)/shard_map/ppermute | solution.py:20
  59.8 1.5 %reduce_sum.58 = f32[4096]{0:T(1024)} reduce(f32[8,4096]{1,0:T(8,128)} %get-tuple-element.12, f32[]{:T(128)} %constant.2.clone.1), dimensions={0}, to_apply=%region_4.0 | reduce | flops 28672 | bytes 147460 | tf_op jit(solution)/shard_map/reduce_sum | solution.py:405
  61.3 1.5 %reduce_sum.59 = f32[4096]{0:T(1024)} reduce(f32[8,4096]{1,0:T(8,128)} %get-tuple-element.13, f32[]{:T(128)} %constant.2.clone.1), dimensions={0}, to_apply=%region_5.0 | reduce | flops 28672 | bytes 147460 | tf_op jit(solution)/shard_map/reduce_sum | solution.py:405
  62.9 0.0 collective-permute-done.1
  62.9 0.1 copy.13
  62.9 0.1 reshape.35
  63.0 0.0 copy-done
  63.0 0.0 copy-start.1
  63.1 3.0 %fusion.3 = bf16[1,128,4096]{2,1,0:T(8,128)(2,1)} fusion(f32[128,4096]{1,0:T(8,128)} %get-tuple-element.10, f32[128]{0:T(128)S(1)} %fusion.5, bf16[1,128,4096]{2,1,0:T(8,128)(2,1)S(1)} %copy-done), kind=kLoop, calls=%fused_computation.8 | loop fusion | flops 2097152 | bytes 4194816 | tf_op jit(solution)/shard_map/broadcast_in_dim | solution.py:409
  66.0 0.0 copy-done.1
  66.0 1.0 %copy.15 = bf16[1,128,4096]{2,1,0:T(8,128)(2,1)} copy(bf16[1,128,4096]{2,1,0:T(8,128)(2,1)S(1)} %bitcast.21) | data formatting | bytes 2097152
  (4 shorter events, 0.0 us)
Async XLA Ops:
  0.6 3.1 %copy-start.2 = (s32[128]{0:T(128)S(1)}, s32[128]{0:T(128)}, u32[]{:S(2)}) copy-start(s32[128]{0:T(128)} %param.9) | copy-start | bytes 1540
  7.7 3.1 %collective-permute-start = (f32[3,128]{1,0:T(4,128)S(1)}, f32[3,128]{1,0:T(4,128)S(1)}, u32[]{:S(2)}, u32[]{:S(2)}) collective-permute-start(f32[3,128]{1,0:T(4,128)S(1)} %pad_maximum_fusion), channel_id=1, source_target_pairs={{0,1},{1,0},{2,3},{3,2},{4,5},{5,4},{6,7},{7,6},{8,9},{9,8},{10,11... | collective-permute-start | bytes 4616 | tf_op jit(solution)/shard_map/ppermute | solution.py:20
  11.5 51.5 %copy-start = (bf16[1,128,4096]{2,1,0:T(8,128)(2,1)S(1)}, bf16[1,128,4096]{2,1,0:T(8,128)(2,1)}, u32[]{:S(2)}) copy-start(bf16[1,128,4096]{2,1,0:T(8,128)(2,1)} %param.12) | copy-start | bytes 3145732
  58.5 4.4 %collective-permute-start.1 = (f32[16,8]{1,0:T(8,128)S(1)}, f32[16,8]{1,0:T(8,128)S(1)}, u32[]{:S(2)}, u32[]{:S(2)}) collective-permute-start(f32[16,8]{1,0:T(8,128)S(1)} %reduce_sum.57), channel_id=1, source_target_pairs={{0,1},{1,0},{2,3},{3,2},{4,5},{5,4},{6,7},{7,6},{8,9},{9,8},{10,11... | collective-permute-start | bytes 1544 | tf_op jit(solution)/shard_map/ppermute | solution.py:20
  63.0 3.0 %copy-start.1 = (bf16[128,4096]{1,0:T(8,128)(2,1)S(1)}, bf16[128,4096]{1,0:T(8,128)(2,1)}, u32[]{:S(2)}) copy-start(bf16[128,4096]{1,0:T(8,128)(2,1)} %get-tuple-element.9) | copy-start | bytes 3145732
